TPU v7x, 256 devices: a whole 4x4x8 slice. The times are simulated.
256 devices in a mesh: sub: 128 (over x_hi, z, y, core), blk: 2 (over x_lo).
Axes of the slice: x: 4 (x_hi: 2, x_lo: 2; x = x_hi * 2 + x_lo), y: 4, z: 8, core: 2. Of those that a mesh axis runs over, the one named last changes fastest.
Arguments:
- source_terms: bfloat16 [2, 105, 2, 32768], P(None, None, None, ('sub', 'blk')), may hold values from -6 to 6
- inverse_blocks: bfloat16 [2, 105, 105, 32768], P(None, None, None, ('sub', 'blk'))
- face_matrices: bfloat16 [4, 105, 105], replicated, may hold values from -0.625 to 0.625
- trace_matrices: bfloat16 [4, 30, 105], replicated, may hold values from -0.625 to 0.625
- neighbours: int32 [32768, 4], P(('sub', 'blk')), may hold values from 0 to 256
- coupling: bfloat16 [32768, 4, 2], P(('sub', 'blk')), may hold values from -0.8984375 to 0.8984375
- slot_faces: int32 [128, 4, 256], P('sub', None, 'blk'), may hold values from 0 to 511
- robin_params: bfloat16 [2, 128, 4, 256], P(None, 'sub', None, 'blk'), may hold values from 0.19921875 to 0.796875
- matching: int32 [4, 128], P(None, 'sub'), may hold values from 0 to 127, as said below
- counts: int32 [4, 128, 2], P(None, 'sub', 'blk'), may hold values from 0 to 128, as said below
Outputs:
- solution: bfloat16 [2, 105, 2, 32768], P(None, None, None, ('sub', 'blk'))
Inputs may be any that keep to these rules, and one draw needn't show every extreme that they name: matching[r, s] is the subdomain paired with s in round r, or s itself when s has none; pairing is mutual and a partner lies at most 2 subdomains away from s. counts[r, s, b] is the same at s's partner in round r, and 0 when s has no partner; slot j of block b of s faces slot j of block b of the partner. slot_faces holds 4 e + f for element e of the slot's block and its face f. neighbours holds an element index within the subdomain; the value 256 means no neighbour across that face.
All inputs are finite; a program needn't handle non-finite values.
Results may differ from a plain program's by a relative error of at most 0.025.
Values may be sent and summed in bfloat16 or wider, within the bound.
A program may use at most 128 MiB of HBM per device.

v0:
```python
import jax
import jax.numpy as jnp
from jax import lax
from jax.sharding import PartitionSpec as P

TDOF = 30
E_DEV = 128
IFACE = 128
ITERS = 2
ROUNDS = 4


def from_behind(value, axis, steps):
    count = lax.axis_size(axis)
    initial, last = (max(0, -steps), min(count, count - steps))
    return lax.ppermute(value, axis, [(source, source + steps) for source in range(initial, last)])


def complex_times(left_re, left_im, right_re, right_im):
    return (left_re * right_re - left_im * right_im, left_re * right_im + left_im * right_re)


def solve_layout(
    sources,
    inverse,
    face_matrices,
    trace_matrices,
    neighbours,
    weights,
    slot_faces,
    robin_params,
    counts,
    matching,
    collect,
):
    sources_held = sources.shape[2]
    elements_held = sources.shape[3]
    slot_count = slot_faces.shape[2]
    slot_index = jnp.arange(slot_count, dtype=jnp.int32)
    owner_block = slot_index // IFACE
    myself = lax.axis_index("sub")
    element_index = jnp.arange(elements_held, dtype=jnp.int32)
    base_terms = sources.astype(jnp.float32)
    weight_re = jnp.transpose(weights[:, :, 0].astype(jnp.float32))
    weight_im = jnp.transpose(weights[:, :, 1].astype(jnp.float32))
    fields = jnp.zeros(sources.shape, jnp.bfloat16)
    interface = jnp.zeros((ROUNDS, 2, TDOF, sources_held, slot_count), jnp.bfloat16)
    lifted = [jnp.zeros(sources.shape, jnp.float32) for colour in range(ROUNDS)]
    for repeat in range(ITERS):
        for colour in range(ROUNDS):
            slot_codes = slot_faces[0, colour]
            element = owner_block * E_DEV + slot_codes // 4
            chosen = jnp.take(trace_matrices, slot_codes % 4, axis=0)
            in_use = slot_index % IFACE < jnp.take(counts[colour, 0], owner_block)
            picked = jnp.take(fields, element, axis=3)
            face_trace = jnp.einsum(
                "jkd,cdsj->cksj", chosen, picked, preferred_element_type=jnp.float32
            )
            robin_re = robin_params[0, 0, colour].astype(jnp.float32)
            robin_im = robin_params[1, 0, colour].astype(jnp.float32)
            scaled_re, scaled_im = complex_times(robin_re, robin_im, face_trace[0], face_trace[1])
            former = interface[colour].astype(jnp.float32)
            outgoing = jnp.stack([2.0 * scaled_re - former[0], 2.0 * scaled_im - former[1]]).astype(
                jnp.bfloat16
            )
            offset = matching[colour, 0] - myself
            arrived = jnp.zeros_like(outgoing)
            for distance in (1, -1, 2, -2):
                shifted = from_behind(outgoing, "sub", distance)
                arrived = jnp.where(offset == -distance, shifted, arrived)
            updated = jnp.where(in_use, arrived, interface[colour])
            interface = interface.at[colour].set(updated)
            slot_lift = jnp.einsum(
                "jkd,cksj->cdsj", chosen, updated, preferred_element_type=jnp.float32
            ).astype(jnp.bfloat16)
            slot_lift = jnp.where(in_use, slot_lift, jnp.zeros_like(slot_lift))
            element_hot = (element[:, None] == element_index[None, :]).astype(jnp.bfloat16)
            lifted[colour] = jnp.einsum(
                "cdsj,je->cdse", slot_lift, element_hot, preferred_element_type=jnp.float32
            )
            gathered = collect(fields)
            padded = jnp.concatenate(
                [gathered, jnp.zeros(gathered.shape[:3] + (1,), jnp.bfloat16)], axis=3
            )
            rhs_sum = base_terms + sum(lifted)
            for face_no in range(4):
                nearby = jnp.take(padded, neighbours[:, face_no], axis=3)
                coupled = jnp.einsum(
                    "kd,cdse->ckse",
                    face_matrices[face_no],
                    nearby,
                    preferred_element_type=jnp.float32,
                )
                flux_re, flux_im = complex_times(
                    weight_re[face_no][None, None, :],
                    weight_im[face_no][None, None, :],
                    coupled[0],
                    coupled[1],
                )
                rhs_sum = rhs_sum + jnp.stack([flux_re, flux_im])
            right_side = rhs_sum.astype(jnp.bfloat16)
            real_part = jnp.einsum(
                "ije,jse->ise", inverse[0], right_side[0], preferred_element_type=jnp.float32
            ) - jnp.einsum(
                "ije,jse->ise", inverse[1], right_side[1], preferred_element_type=jnp.float32
            )
            imag_part = jnp.einsum(
                "ije,jse->ise", inverse[0], right_side[1], preferred_element_type=jnp.float32
            ) + jnp.einsum(
                "ije,jse->ise", inverse[1], right_side[0], preferred_element_type=jnp.float32
            )
            fields = jnp.stack([real_part, imag_part]).astype(jnp.bfloat16)
    return fields


def shards(
    source_terms,
    inverse_blocks,
    face_matrices,
    trace_matrices,
    neighbours,
    coupling,
    slot_faces,
    robin_params,
    matching,
    counts,
):

    def gather_fields(values):
        return lax.all_gather(values, "blk", axis=3, tiled=True)

    return solve_layout(
        source_terms,
        inverse_blocks,
        face_matrices,
        trace_matrices,
        neighbours,
        coupling,
        slot_faces,
        robin_params,
        counts,
        matching,
        gather_fields,
    )


def solution(mesh):
    in_specs = (
        P(None, None, None, ("sub", "blk")),
        P(None, None, None, ("sub", "blk")),
        P(),
        P(),
        P(("sub", "blk"), None),
        P(("sub", "blk"), None, None),
        P("sub", None, "blk"),
        P(None, "sub", None, "blk"),
        P(None, "sub"),
        P(None, "sub", "blk"),
    )
    out_specs = P(None, None, None, ("sub", "blk"))
    return jax.shard_map(shards, mesh=mesh, in_specs=in_specs, out_specs=out_specs, check_vma=False)
```

profile of v0, /device:TPU:6, one launch (start us, length us, event | category | flops | bytes accessed | tf_op | source)
XLA Modules:
  0.0 501.5 jit_solution(3375504782587574543)
XLA Ops:
  2.1 4.3 gather_fusion.1
  10.2 11.0 %collective-permute-start = (bf16[2,30,2,128]{3,2,1,0:T(2,128)(2,1)}, bf16[2,30,2,128]{3,2,1,0:T(2,128)(2,1)}, u32[]{:S(2)}, u32[]{:S(2)}) collective-permute-start(bf16[2,30,2,128]{3,2,1,0:T(2,128)(2,1)} %pad_maximum_fusion.8), channel_id=1, source_target_pairs={{4,0},{6,2},{8,4},{10,6},{12,8},{14,10},{16,12},{18,14},{20,16},{2... | collective-permute-start | bytes 92168 | tf_op jit(solution)/shard_map/ppermute | solution.py:16
  23.1 8.5 %collective-permute-start.2 = (bf16[2,30,2,128]{3,2,1,0:T(2,128)(2,1)}, bf16[2,30,2,128]{3,2,1,0:T(2,128)(2,1)}, u32[]{:S(2)}, u32[]{:S(2)}) collective-permute-start(bf16[2,30,2,128]{3,2,1,0:T(2,128)(2,1)} %pad_maximum_fusion.8), channel_id=1, source_target_pairs={{2,0},{4,2},{6,4},{8,6},{10,8},{12,10},{14,12},{16,14},{18,16},{20... | collective-permute-start | bytes 92168 | tf_op jit(solution)/shard_map/ppermute | solution.py:16
  41.8 13.0 %fusion.436 = (bf16[1,105,105,128]{3,0,2,1:T(2,128)(2,1)}, bf16[1,105,105,128]{3,0,2,1:T(2,128)(2,1)}) fusion(bf16[2,105,105,128]{3,0,2,1:T(2,128)(2,1)} %param.33), kind=kLoop, calls=%fused_computation.720 | loop fusion | bytes 11289600 | tf_op jit(solution)/shard_map/slice | solution.py:103
  55.5 4.3 gather_fusion.7
  62.1 4.3 gather_fusion.13
  68.3 4.3 gather_fusion.19
  84.9 10.6 %copy.580 = bf16[1,105,105,128]{2,1,3,0:T(8,128)(2,1)} copy(bf16[1,105,105,128]{3,0,2,1:T(2,128)(2,1)} %get-tuple-element.132) | data formatting | bytes 5644800
  95.5 10.6 %copy.579 = bf16[1,105,105,128]{2,1,3,0:T(8,128)(2,1)} copy(bf16[1,105,105,128]{3,0,2,1:T(2,128)(2,1)} %get-tuple-element.131) | data formatting | bytes 5644800
  108.7 4.2 fusion.30
  114.9 2.0 fusion.182
  121.4 3.5 collective-permute-start.4
  124.9 2.3 collective-permute-start.5
  127.3 14.5 %collective-permute-start.6 = (bf16[2,30,2,128]{3,2,1,0:T(2,128)(2,1)S(1)}, bf16[2,30,2,128]{3,2,1,0:T(2,128)(2,1)S(1)}, u32[]{:S(2)}, u32[]{:S(2)}) collective-permute-start(bf16[2,30,2,128]{3,2,1,0:T(2,128)(2,1)S(1)} %pad_maximum_fusion.9), channel_id=1, source_target_pairs={{2,0},{4,2},{6,4},{8,6},{10,8},{12,10},{14,12},{16,14},{18,16},{20... | collective-permute-start | bytes 92168 | tf_op jit(solution)/shard_map/ppermute | solution.py:16
  143.7 5.8 %all_gather.25 = bf16[2,105,2,256]{1,2,3,0:T(2,128)(2,1)S(1)} all-gather(bf16[2,105,2,128]{1,2,3,0:T(2,128)(2,1)S(1)} %pad_maximum_fusion), channel_id=1, replica_groups=mesh['sub'=128,'blk'=2] {'blk'}, dimensions={3}, use_global_device_ids=true | all-gather | bytes 322560 | tf_op jit(solution)/shard_map/all_gather | solution.py:130
  164.4 4.0 fusion.26
  168.6 4.2 fusion.24
  179.3 7.5 %collective-permute-start.10 = (bf16[2,30,2,128]{3,2,1,0:T(2,128)(2,1)S(1)}, bf16[2,30,2,128]{3,2,1,0:T(2,128)(2,1)S(1)}, u32[]{:S(2)}, u32[]{:S(2)}) collective-permute-start(bf16[2,30,2,128]{3,2,1,0:T(2,128)(2,1)S(1)} %pad_maximum_fusion.10), channel_id=1, source_target_pairs={{2,0},{4,2},{6,4},{8,6},{10,8},{12,10},{14,12},{16,14},{18,16},{20... | collective-permute-start | bytes 92168 | tf_op jit(solution)/shard_map/ppermute | solution.py:16
  188.8 2.3 collective-permute-start.8
  191.1 3.5 collective-permute-start.9
  194.6 5.9 %all_gather.26 = bf16[2,105,2,256]{1,2,3,0:T(2,128)(2,1)S(1)} all-gather(bf16[2,105,2,128]{1,2,3,0:T(2,128)(2,1)S(1)} %pad_maximum_fusion.1), channel_id=1, replica_groups=mesh['sub'=128,'blk'=2] {'blk'}, dimensions={3}, use_global_device_ids=true | all-gather | bytes 322560 | tf_op jit(solution)/shard_map/all_gather | solution.py:130
  219.1 4.0 fusion.22
  223.3 4.2 fusion.20
  227.5 2.0 fusion.194
  234.0 8.0 %collective-permute-start.12 = (bf16[2,30,2,128]{3,2,1,0:T(2,128)(2,1)S(1)}, bf16[2,30,2,128]{3,2,1,0:T(2,128)(2,1)S(1)}, u32[]{:S(2)}, u32[]{:S(2)}) collective-permute-start(bf16[2,30,2,128]{3,2,1,0:T(2,128)(2,1)S(1)} %pad_maximum_fusion.11), channel_id=1, source_target_pairs={{4,0},{6,2},{8,4},{10,6},{12,8},{14,10},{16,12},{18,14},{20,16},{2... | collective-permute-start | bytes 92168 | tf_op jit(solution)/shard_map/ppermute | solution.py:16
  244.0 14.4 %collective-permute-start.14 = (bf16[2,30,2,128]{3,2,1,0:T(2,128)(2,1)S(1)}, bf16[2,30,2,128]{3,2,1,0:T(2,128)(2,1)S(1)}, u32[]{:S(2)}, u32[]{:S(2)}) collective-permute-start(bf16[2,30,2,128]{3,2,1,0:T(2,128)(2,1)S(1)} %pad_maximum_fusion.11), channel_id=1, source_target_pairs={{2,0},{4,2},{6,4},{8,6},{10,8},{12,10},{14,12},{16,14},{18,16},{20... | collective-permute-start | bytes 92168 | tf_op jit(solution)/shard_map/ppermute | solution.py:16
  260.4 6.0 %all_gather.27 = bf16[2,105,2,256]{1,2,3,0:T(2,128)(2,1)S(1)} all-gather(bf16[2,105,2,128]{1,2,3,0:T(2,128)(2,1)S(1)} %pad_maximum_fusion.2), channel_id=1, replica_groups=mesh['sub'=128,'blk'=2] {'blk'}, dimensions={3}, use_global_device_ids=true | all-gather | bytes 322560 | tf_op jit(solution)/shard_map/all_gather | solution.py:130
  276.5 4.0 fusion.18
  280.7 4.2 fusion.16
  284.9 2.0 fusion.200
  290.2 2.1 fusion.249
  292.6 3.1 collective-permute-start.16
  295.7 2.8 collective-permute-start.17
  298.5 13.4 %collective-permute-start.18 = (bf16[2,30,2,128]{3,2,1,0:T(2,128)(2,1)S(1)}, bf16[2,30,2,128]{3,2,1,0:T(2,128)(2,1)}, u32[]{:S(2)}, u32[]{:S(2)}) collective-permute-start(bf16[2,30,2,128]{3,2,1,0:T(2,128)(2,1)S(1)} %pad_maximum_fusion.12), channel_id=1, source_target_pairs={{2,0},{4,2},{6,4},{8,6},{10,8},{12,10},{14,12},{16,14},{18,16},{20... | collective-permute-start | bytes 92168 | tf_op jit(solution)/shard_map/ppermute | solution.py:16
  313.8 5.8 %all_gather.28 = bf16[2,105,2,256]{1,2,3,0:T(2,128)(2,1)S(1)} all-gather(bf16[2,105,2,128]{1,2,3,0:T(2,128)(2,1)S(1)} %pad_maximum_fusion.3), channel_id=1, replica_groups=mesh['sub'=128,'blk'=2] {'blk'}, dimensions={3}, use_global_device_ids=true | all-gather | bytes 322560 | tf_op jit(solution)/shard_map/all_gather | solution.py:130
  328.5 2.1 fusion.79
  331.1 4.0 fusion.14
  335.3 4.2 fusion.12
  339.4 2.0 fusion.206
  344.8 2.1 fusion.243
  347.8 2.3 collective-permute-start.20
  350.1 3.5 collective-permute-start.21
  353.6 13.4 %collective-permute-start.22 = (bf16[2,30,2,128]{3,2,1,0:T(2,128)(2,1)}, bf16[2,30,2,128]{3,2,1,0:T(2,128)(2,1)}, u32[]{:S(2)}, u32[]{:S(2)}) collective-permute-start(bf16[2,30,2,128]{3,2,1,0:T(2,128)(2,1)} %pad_maximum_fusion.13), channel_id=1, source_target_pairs={{2,0},{4,2},{6,4},{8,6},{10,8},{12,10},{14,12},{16,14},{18,16},{20... | collective-permute-start | bytes 92168 | tf_op jit(solution)/shard_map/ppermute | solution.py:16
  368.9 5.9 %all_gather.29 = bf16[2,105,2,256]{1,2,3,0:T(2,128)(2,1)S(1)} all-gather(bf16[2,105,2,128]{1,2,3,0:T(2,128)(2,1)S(1)} %pad_maximum_fusion.4), channel_id=1, replica_groups=mesh['sub'=128,'blk'=2] {'blk'}, dimensions={3}, use_global_device_ids=true | all-gather | bytes 322560 | tf_op jit(solution)/shard_map/all_gather | solution.py:130
  382.1 2.1 fusion.81
  385.3 4.0 fusion.10
  389.5 4.2 fusion.8
  393.7 2.0 fusion.212
  399.0 2.1 fusion.237
  401.4 2.3 collective-permute-start.24
  403.7 3.6 collective-permute-start.25
  407.3 13.4 %collective-permute-start.26 = (bf16[2,30,2,128]{3,2,1,0:T(2,128)(2,1)S(1)}, bf16[2,30,2,128]{3,2,1,0:T(2,128)(2,1)S(1)}, u32[]{:S(2)}, u32[]{:S(2)}) collective-permute-start(bf16[2,30,2,128]{3,2,1,0:T(2,128)(2,1)S(1)} %pad_maximum_fusion.14), channel_id=1, source_target_pairs={{2,0},{4,2},{6,4},{8,6},{10,8},{12,10},{14,12},{16,14},{18,16},{20... | collective-permute-start | bytes 92168 | tf_op jit(solution)/shard_map/ppermute | solution.py:16
  422.6 5.9 %all_gather.30 = bf16[2,105,2,256]{1,2,3,0:T(2,128)(2,1)S(1)} all-gather(bf16[2,105,2,128]{1,2,3,0:T(2,128)(2,1)S(1)} %pad_maximum_fusion.5), channel_id=1, replica_groups=mesh['sub'=128,'blk'=2] {'blk'}, dimensions={3}, use_global_device_ids=true | all-gather | bytes 322560 | tf_op jit(solution)/shard_map/all_gather | solution.py:130
  435.1 2.1 fusion.83
  437.7 4.0 fusion.6
  441.8 4.2 fusion.4
  446.0 2.0 fusion.218
  452.5 2.3 collective-permute-start.28
  454.9 3.5 collective-permute-start.29
  458.4 13.4 %collective-permute-start.30 = (bf16[2,30,2,128]{3,2,1,0:T(2,128)(2,1)S(1)}, bf16[2,30,2,128]{3,2,1,0:T(2,128)(2,1)S(1)}, u32[]{:S(2)}, u32[]{:S(2)}) collective-permute-start(bf16[2,30,2,128]{3,2,1,0:T(2,128)(2,1)S(1)} %pad_maximum_fusion.15), channel_id=1, source_target_pairs={{2,0},{4,2},{6,4},{8,6},{10,8},{12,10},{14,12},{16,14},{18,16},{20... | collective-permute-start | bytes 92168 | tf_op jit(solution)/shard_map/ppermute | solution.py:16
  473.7 5.9 %all_gather.31 = bf16[2,105,2,256]{1,2,3,0:T(2,128)(2,1)S(1)} all-gather(bf16[2,105,2,128]{1,2,3,0:T(2,128)(2,1)S(1)} %pad_maximum_fusion.6), channel_id=1, replica_groups=mesh['sub'=128,'blk'=2] {'blk'}, dimensions={3}, use_global_device_ids=true | all-gather | bytes 322560 | tf_op jit(solution)/shard_map/all_gather | solution.py:130
  487.6 4.0 fusion.2
  491.8 4.2 fusion
  495.9 2.0 fusion.224
  (525 shorter events, 162.0 us)
Async XLA Ops:
  1.5 53.4 %copy-start.53 = (s32[128]{0:T(128)}, s32[128]{0:T(128)S(1)}, u32[]{:S(2)}) copy-start(s32[128]{0:T(128)S(1)} %get-tuple-element.245) | copy-start | bytes 1540
  1.5 53.4 %copy-start.56 = (s32[128]{0:T(128)}, s32[128]{0:T(128)S(1)}, u32[]{:S(2)}) copy-start(s32[128]{0:T(128)S(1)} %get-tuple-element.251) | copy-start | bytes 1540
  6.5 32.6 %copy-start.20 = (bf16[4,105,105]{2,0,1:T(4,128)(2,1)S(1)}, bf16[4,105,105]{2,0,1:T(4,128)(2,1)}, u32[]{:S(2)}) copy-start(bf16[4,105,105]{2,0,1:T(4,128)(2,1)} %param.34) | copy-start | bytes 264604
  6.6 33.4 %copy-start.62 = (bf16[128,4,2]{0,2,1:T(2,128)(2,1)S(1)}, bf16[128,4,2]{0,2,1:T(2,128)(2,1)}, u32[]{:S(2)}) copy-start(bf16[128,4,2]{0,2,1:T(2,128)(2,1)} %param.37) | copy-start | bytes 6148
  6.7 48.1 %copy-start.15 = (bf16[128,30,105,1]{2,0,1,3:T(8,128)(2,1)}, bf16[128,30,105,1]{2,0,1,3:T(8,128)(2,1)S(1)}, u32[]{:S(2)}) copy-start(bf16[128,30,105,1]{2,0,1,3:T(8,128)(2,1)S(1)} %select_bitcast_fusion.3) | copy-start | bytes 2419204
  9.4 45.4 %copy-start.78 = (f32[128]{0:T(128)}, f32[128]{0:T(128)S(1)}, u32[]{:S(2)}) copy-start(f32[128]{0:T(128)S(1)} %get-tuple-element.241) | copy-start | bytes 1540
  9.5 45.4 %copy-start.80 = (f32[128]{0:T(128)}, f32[128]{0:T(128)S(1)}, u32[]{:S(2)}) copy-start(f32[128]{0:T(128)S(1)} %get-tuple-element.242) | copy-start | bytes 1540
  10.2 96.0 %collective-permute-start = (bf16[2,30,2,128]{3,2,1,0:T(2,128)(2,1)}, bf16[2,30,2,128]{3,2,1,0:T(2,128)(2,1)}, u32[]{:S(2)}, u32[]{:S(2)}) collective-permute-start(bf16[2,30,2,128]{3,2,1,0:T(2,128)(2,1)} %pad_maximum_fusion.8), channel_id=1, source_target_pairs={{4,0},{6,2},{8,4},{10,6},{12,8},{14,10},{16,12},{18,14},{20,16},{2... | collective-permute-start | bytes 92168 | tf_op jit(solution)/shard_map/ppermute | solution.py:16
  21.2 84.9 %collective-permute-start.1 = (bf16[2,30,2,128]{3,2,1,0:T(2,128)(2,1)}, bf16[2,30,2,128]{3,2,1,0:T(2,128)(2,1)}, u32[]{:S(2)}, u32[]{:S(2)}) collective-permute-start(bf16[2,30,2,128]{3,2,1,0:T(2,128)(2,1)} %pad_maximum_fusion.8), channel_id=1, source_target_pairs={{0,4},{2,6},{4,8},{6,10},{8,12},{10,14},{12,16},{14,18},{16,20},{1... | collective-permute-start | bytes 92168 | tf_op jit(solution)/shard_map/ppermute | solution.py:16
  23.1 83.0 %collective-permute-start.2 = (bf16[2,30,2,128]{3,2,1,0:T(2,128)(2,1)}, bf16[2,30,2,128]{3,2,1,0:T(2,128)(2,1)}, u32[]{:S(2)}, u32[]{:S(2)}) collective-permute-start(bf16[2,30,2,128]{3,2,1,0:T(2,128)(2,1)} %pad_maximum_fusion.8), channel_id=1, source_target_pairs={{2,0},{4,2},{6,4},{8,6},{10,8},{12,10},{14,12},{16,14},{18,16},{20... | collective-permute-start | bytes 92168 | tf_op jit(solution)/shard_map/ppermute | solution.py:16
  31.7 74.5 %collective-permute-start.3 = (bf16[2,30,2,128]{3,2,1,0:T(2,128)(2,1)}, bf16[2,30,2,128]{3,2,1,0:T(2,128)(2,1)}, u32[]{:S(2)}, u32[]{:S(2)}) collective-permute-start(bf16[2,30,2,128]{3,2,1,0:T(2,128)(2,1)} %pad_maximum_fusion.8), channel_id=1, source_target_pairs={{0,2},{2,4},{4,6},{6,8},{8,10},{10,12},{12,14},{14,16},{16,18},{18... | collective-permute-start | bytes 92168 | tf_op jit(solution)/shard_map/ppermute | solution.py:16
  36.2 37.3 %copy-start.35 = (pred[128]{0:T(512)(128)(4,1)}, pred[128]{0:T(512)(128)(4,1)S(1)}, u32[]{:S(2)}) copy-start(pred[128]{0:T(512)(128)(4,1)S(1)} %get-tuple-element.265) | copy-start | bytes 388
  36.2 37.3 %copy-start.40 = (pred[128]{0:T(512)(128)(4,1)}, pred[128]{0:T(512)(128)(4,1)S(1)}, u32[]{:S(2)}) copy-start(pred[128]{0:T(512)(128)(4,1)S(1)} %get-tuple-element.116) | copy-start | bytes 388
  36.2 120.0 %copy-start.31 = (pred[128]{0:T(512)(128)(4,1)}, pred[128]{0:T(512)(128)(4,1)S(1)}, u32[]{:S(2)}) copy-start(pred[128]{0:T(512)(128)(4,1)S(1)} %get-tuple-element.261) | copy-start | bytes 388
  36.2 122.1 %copy-start.27 = (pred[128]{0:T(512)(128)(4,1)}, pred[128]{0:T(512)(128)(4,1)S(1)}, u32[]{:S(2)}) copy-start(pred[128]{0:T(512)(128)(4,1)S(1)} %get-tuple-element.263) | copy-start | bytes 388
  80.8 152.0 %copy-start.12 = (bf16[128,30,105,1]{2,0,1,3:T(8,128)(2,1)}, bf16[128,30,105,1]{2,0,1,3:T(8,128)(2,1)S(1)}, u32[]{:S(2)}) copy-start(bf16[128,30,105,1]{2,0,1,3:T(8,128)(2,1)S(1)} %select_bitcast_fusion) | copy-start | bytes 2419204
  116.9 37.8 %copy-start.41 = (pred[128]{0:T(512)(128)(4,1)S(1)}, pred[128]{0:T(512)(128)(4,1)}, u32[]{:S(2)}) copy-start(pred[128]{0:T(512)(128)(4,1)} %copy-done.40) | copy-start | bytes 388
  118.9 36.3 %copy-start.36 = (pred[128]{0:T(512)(128)(4,1)S(1)}, pred[128]{0:T(512)(128)(4,1)}, u32[]{:S(2)}) copy-start(pred[128]{0:T(512)(128)(4,1)} %copy-done.35) | copy-start | bytes 388
  121.1 38.4 %copy-start.86 = (pred[128]{0:T(512)(128)(4,1)S(1)}, pred[128]{0:T(512)(128)(4,1)}, u32[]{:S(2)}) copy-start(pred[128]{0:T(512)(128)(4,1)} %select_compare_fusion.2) | copy-start | bytes 388
  121.4 38.1 %collective-permute-start.4 = (bf16[2,30,2,128]{3,2,1,0:T(2,128)(2,1)S(1)}, bf16[2,30,2,128]{3,2,1,0:T(2,128)(2,1)S(1)}, u32[]{:S(2)}, u32[]{:S(2)}) collective-permute-start(bf16[2,30,2,128]{3,2,1,0:T(2,128)(2,1)S(1)} %pad_maximum_fusion.9), channel_id=1, source_target_pairs={{4,0},{6,2},{8,4},{10,6},{12,8},{14,10},{16,12},{18,14},{20,16},{2... | collective-permute-start | bytes 92168 | tf_op jit(solution)/shard_map/ppermute | solution.py:16
  124.9 34.6 %collective-permute-start.5 = (bf16[2,30,2,128]{3,2,1,0:T(2,128)(2,1)S(1)}, bf16[2,30,2,128]{3,2,1,0:T(2,128)(2,1)S(1)}, u32[]{:S(2)}, u32[]{:S(2)}) collective-permute-start(bf16[2,30,2,128]{3,2,1,0:T(2,128)(2,1)S(1)} %pad_maximum_fusion.9), channel_id=1, source_target_pairs={{0,4},{2,6},{4,8},{6,10},{8,12},{10,14},{12,16},{14,18},{16,20},{1... | collective-permute-start | bytes 92168 | tf_op jit(solution)/shard_map/ppermute | solution.py:16
  127.3 32.3 %collective-permute-start.6 = (bf16[2,30,2,128]{3,2,1,0:T(2,128)(2,1)S(1)}, bf16[2,30,2,128]{3,2,1,0:T(2,128)(2,1)S(1)}, u32[]{:S(2)}, u32[]{:S(2)}) collective-permute-start(bf16[2,30,2,128]{3,2,1,0:T(2,128)(2,1)S(1)} %pad_maximum_fusion.9), channel_id=1, source_target_pairs={{2,0},{4,2},{6,4},{8,6},{10,8},{12,10},{14,12},{16,14},{18,16},{20... | collective-permute-start | bytes 92168 | tf_op jit(solution)/shard_map/ppermute | solution.py:16
  141.8 17.7 %collective-permute-start.7 = (bf16[2,30,2,128]{3,2,1,0:T(2,128)(2,1)S(1)}, bf16[2,30,2,128]{3,2,1,0:T(2,128)(2,1)}, u32[]{:S(2)}, u32[]{:S(2)}) collective-permute-start(bf16[2,30,2,128]{3,2,1,0:T(2,128)(2,1)S(1)} %pad_maximum_fusion.9), channel_id=1, source_target_pairs={{0,2},{2,4},{4,6},{6,8},{8,10},{10,12},{12,14},{14,16},{16,18},{18... | collective-permute-start | bytes 92168 | tf_op jit(solution)/shard_map/ppermute | solution.py:16
  176.8 34.2 %copy-start.32 = (pred[128]{0:T(512)(128)(4,1)S(1)}, pred[128]{0:T(512)(128)(4,1)}, u32[]{:S(2)}) copy-start(pred[128]{0:T(512)(128)(4,1)} %copy-done.31) | copy-start | bytes 388
  178.1 35.0 %copy-start.28 = (pred[128]{0:T(512)(128)(4,1)S(1)}, pred[128]{0:T(512)(128)(4,1)}, u32[]{:S(2)}) copy-start(pred[128]{0:T(512)(128)(4,1)} %copy-done.27) | copy-start | bytes 388
  179.0 35.8 %copy-start.19 = (bf16[4,2,30,2,128]{4,3,2,1,0:T(2,128)(2,1)S(1)}, bf16[4,2,30,2,128]{4,3,2,1,0:T(2,128)(2,1)}, u32[]{:S(2)}) copy-start(bf16[4,2,30,2,128]{4,3,2,1,0:T(2,128)(2,1)} %copy-done.18) | copy-start | bytes 368644
  179.0 35.8 %copy-start.84 = (pred[128]{0:T(512)(128)(4,1)S(1)}, pred[128]{0:T(512)(128)(4,1)}, u32[]{:S(2)}) copy-start(pred[128]{0:T(512)(128)(4,1)} %select_compare_fusion.1) | copy-start | bytes 388
  179.3 34.9 %collective-permute-start.10 = (bf16[2,30,2,128]{3,2,1,0:T(2,128)(2,1)S(1)}, bf16[2,30,2,128]{3,2,1,0:T(2,128)(2,1)S(1)}, u32[]{:S(2)}, u32[]{:S(2)}) collective-permute-start(bf16[2,30,2,128]{3,2,1,0:T(2,128)(2,1)S(1)} %pad_maximum_fusion.10), channel_id=1, source_target_pairs={{2,0},{4,2},{6,4},{8,6},{10,8},{12,10},{14,12},{16,14},{18,16},{20... | collective-permute-start | bytes 92168 | tf_op jit(solution)/shard_map/ppermute | solution.py:16
  186.8 27.4 %collective-permute-start.11 = (bf16[2,30,2,128]{3,2,1,0:T(2,128)(2,1)S(1)}, bf16[2,30,2,128]{3,2,1,0:T(2,128)(2,1)S(1)}, u32[]{:S(2)}, u32[]{:S(2)}) collective-permute-start(bf16[2,30,2,128]{3,2,1,0:T(2,128)(2,1)S(1)} %pad_maximum_fusion.10), channel_id=1, source_target_pairs={{0,2},{2,4},{4,6},{6,8},{8,10},{10,12},{12,14},{14,16},{16,18},{18... | collective-permute-start | bytes 92168 | tf_op jit(solution)/shard_map/ppermute | solution.py:16
  188.8 25.5 %collective-permute-start.8 = (bf16[2,30,2,128]{3,2,1,0:T(2,128)(2,1)S(1)}, bf16[2,30,2,128]{3,2,1,0:T(2,128)(2,1)S(1)}, u32[]{:S(2)}, u32[]{:S(2)}) collective-permute-start(bf16[2,30,2,128]{3,2,1,0:T(2,128)(2,1)S(1)} %pad_maximum_fusion.10), channel_id=1, source_target_pairs={{4,0},{6,2},{8,4},{10,6},{12,8},{14,10},{16,12},{18,14},{20,16},{2... | collective-permute-start | bytes 92168 | tf_op jit(solution)/shard_map/ppermute | solution.py:16
  191.1 23.8 %collective-permute-start.9 = (bf16[2,30,2,128]{3,2,1,0:T(2,128)(2,1)S(1)}, bf16[2,30,2,128]{3,2,1,0:T(2,128)(2,1)}, u32[]{:S(2)}, u32[]{:S(2)}) collective-permute-start(bf16[2,30,2,128]{3,2,1,0:T(2,128)(2,1)S(1)} %pad_maximum_fusion.10), channel_id=1, source_target_pairs={{0,4},{2,6},{4,8},{6,10},{8,12},{10,14},{12,16},{14,18},{16,20},{1... | collective-permute-start | bytes 92168 | tf_op jit(solution)/shard_map/ppermute | solution.py:16
  232.8 40.9 %copy-start.29 = (pred[128]{0:T(512)(128)(4,1)S(1)}, pred[128]{0:T(512)(128)(4,1)}, u32[]{:S(2)}) copy-start(pred[128]{0:T(512)(128)(4,1)} %copy-done.27) | copy-start | bytes 388
  233.7 40.5 %copy-start.82 = (pred[128]{0:T(512)(128)(4,1)S(1)}, pred[128]{0:T(512)(128)(4,1)}, u32[]{:S(2)}) copy-start(pred[128]{0:T(512)(128)(4,1)} %select_compare_fusion) | copy-start | bytes 388
  233.7 41.4 %copy-start.13 = (bf16[128,30,105,1]{2,0,1,3:T(8,128)(2,1)S(1)}, bf16[128,30,105,1]{2,0,1,3:T(8,128)(2,1)}, u32[]{:S(2)}) copy-start(bf16[128,30,105,1]{2,0,1,3:T(8,128)(2,1)} %copy-done.12) | copy-start | bytes 2419204
  234.0 40.2 %collective-permute-start.12 = (bf16[2,30,2,128]{3,2,1,0:T(2,128)(2,1)S(1)}, bf16[2,30,2,128]{3,2,1,0:T(2,128)(2,1)S(1)}, u32[]{:S(2)}, u32[]{:S(2)}) collective-permute-start(bf16[2,30,2,128]{3,2,1,0:T(2,128)(2,1)S(1)} %pad_maximum_fusion.11), channel_id=1, source_target_pairs={{4,0},{6,2},{8,4},{10,6},{12,8},{14,10},{16,12},{18,14},{20,16},{2... | collective-permute-start | bytes 92168 | tf_op jit(solution)/shard_map/ppermute | solution.py:16
  242.1 32.2 %collective-permute-start.13 = (bf16[2,30,2,128]{3,2,1,0:T(2,128)(2,1)S(1)}, bf16[2,30,2,128]{3,2,1,0:T(2,128)(2,1)S(1)}, u32[]{:S(2)}, u32[]{:S(2)}) collective-permute-start(bf16[2,30,2,128]{3,2,1,0:T(2,128)(2,1)S(1)} %pad_maximum_fusion.11), channel_id=1, source_target_pairs={{0,4},{2,6},{4,8},{6,10},{8,12},{10,14},{12,16},{14,18},{16,20},{1... | collective-permute-start | bytes 92168 | tf_op jit(solution)/shard_map/ppermute | solution.py:16
  244.0 30.2 %collective-permute-start.14 = (bf16[2,30,2,128]{3,2,1,0:T(2,128)(2,1)S(1)}, bf16[2,30,2,128]{3,2,1,0:T(2,128)(2,1)S(1)}, u32[]{:S(2)}, u32[]{:S(2)}) collective-permute-start(bf16[2,30,2,128]{3,2,1,0:T(2,128)(2,1)S(1)} %pad_maximum_fusion.11), channel_id=1, source_target_pairs={{2,0},{4,2},{6,4},{8,6},{10,8},{12,10},{14,12},{16,14},{18,16},{20... | collective-permute-start | bytes 92168 | tf_op jit(solution)/shard_map/ppermute | solution.py:16
  258.4 15.8 %collective-permute-start.15 = (bf16[2,30,2,128]{3,2,1,0:T(2,128)(2,1)S(1)}, bf16[2,30,2,128]{3,2,1,0:T(2,128)(2,1)}, u32[]{:S(2)}, u32[]{:S(2)}) collective-permute-start(bf16[2,30,2,128]{3,2,1,0:T(2,128)(2,1)S(1)} %pad_maximum_fusion.11), channel_id=1, source_target_pairs={{0,2},{2,4},{4,6},{6,8},{8,10},{10,12},{12,14},{14,16},{16,18},{18... | collective-permute-start | bytes 92168 | tf_op jit(solution)/shard_map/ppermute | solution.py:16
  286.9 37.8 %copy-start.43 = (pred[128]{0:T(512)(128)(4,1)S(1)}, pred[128]{0:T(512)(128)(4,1)}, u32[]{:S(2)}) copy-start(pred[128]{0:T(512)(128)(4,1)} %copy-done.40) | copy-start | bytes 388
  288.9 36.2 %copy-start.38 = (pred[128]{0:T(512)(128)(4,1)S(1)}, pred[128]{0:T(512)(128)(4,1)}, u32[]{:S(2)}) copy-start(pred[128]{0:T(512)(128)(4,1)} %copy-done.35) | copy-start | bytes 388
  288.9 37.6 %copy-start.33 = (pred[128]{0:T(512)(128)(4,1)S(1)}, pred[128]{0:T(512)(128)(4,1)}, u32[]{:S(2)}) copy-start(pred[128]{0:T(512)(128)(4,1)} %copy-done.31) | copy-start | bytes 388
  292.3 35.2 %copy-start.88 = (pred[128]{0:T(512)(128)(4,1)S(1)}, pred[128]{0:T(512)(128)(4,1)}, u32[]{:S(2)}) copy-start(pred[128]{0:T(512)(128)(4,1)} %select_compare_fusion.3) | copy-start | bytes 388
  292.6 34.8 %collective-permute-start.16 = (bf16[2,30,2,128]{3,2,1,0:T(2,128)(2,1)S(1)}, bf16[2,30,2,128]{3,2,1,0:T(2,128)(2,1)S(1)}, u32[]{:S(2)}, u32[]{:S(2)}) collective-permute-start(bf16[2,30,2,128]{3,2,1,0:T(2,128)(2,1)S(1)} %pad_maximum_fusion.12), channel_id=1, source_target_pairs={{4,0},{6,2},{8,4},{10,6},{12,8},{14,10},{16,12},{18,14},{20,16},{2... | collective-permute-start | bytes 92168 | tf_op jit(solution)/shard_map/ppermute | solution.py:16
  295.7 31.8 %collective-permute-start.17 = (bf16[2,30,2,128]{3,2,1,0:T(2,128)(2,1)S(1)}, bf16[2,30,2,128]{3,2,1,0:T(2,128)(2,1)S(1)}, u32[]{:S(2)}, u32[]{:S(2)}) collective-permute-start(bf16[2,30,2,128]{3,2,1,0:T(2,128)(2,1)S(1)} %pad_maximum_fusion.12), channel_id=1, source_target_pairs={{0,4},{2,6},{4,8},{6,10},{8,12},{10,14},{12,16},{14,18},{16,20},{1... | collective-permute-start | bytes 92168 | tf_op jit(solution)/shard_map/ppermute | solution.py:16
  298.5 29.0 %collective-permute-start.18 = (bf16[2,30,2,128]{3,2,1,0:T(2,128)(2,1)S(1)}, bf16[2,30,2,128]{3,2,1,0:T(2,128)(2,1)}, u32[]{:S(2)}, u32[]{:S(2)}) collective-permute-start(bf16[2,30,2,128]{3,2,1,0:T(2,128)(2,1)S(1)} %pad_maximum_fusion.12), channel_id=1, source_target_pairs={{2,0},{4,2},{6,4},{8,6},{10,8},{12,10},{14,12},{16,14},{18,16},{20... | collective-permute-start | bytes 92168 | tf_op jit(solution)/shard_map/ppermute | solution.py:16
  311.9 15.6 %collective-permute-start.19 = (bf16[2,30,2,128]{3,2,1,0:T(2,128)(2,1)S(1)}, bf16[2,30,2,128]{3,2,1,0:T(2,128)(2,1)}, u32[]{:S(2)}, u32[]{:S(2)}) collective-permute-start(bf16[2,30,2,128]{3,2,1,0:T(2,128)(2,1)S(1)} %pad_maximum_fusion.12), channel_id=1, source_target_pairs={{0,2},{2,4},{4,6},{6,8},{8,10},{10,12},{12,14},{14,16},{16,18},{18... | collective-permute-start | bytes 92168 | tf_op jit(solution)/shard_map/ppermute | solution.py:16
  347.8 33.3 %collective-permute-start.20 = (bf16[2,30,2,128]{3,2,1,0:T(2,128)(2,1)}, bf16[2,30,2,128]{3,2,1,0:T(2,128)(2,1)S(1)}, u32[]{:S(2)}, u32[]{:S(2)}) collective-permute-start(bf16[2,30,2,128]{3,2,1,0:T(2,128)(2,1)} %pad_maximum_fusion.13), channel_id=1, source_target_pairs={{4,0},{6,2},{8,4},{10,6},{12,8},{14,10},{16,12},{18,14},{20,16},{2... | collective-permute-start | bytes 92168 | tf_op jit(solution)/shard_map/ppermute | solution.py:16
  350.1 31.0 %collective-permute-start.21 = (bf16[2,30,2,128]{3,2,1,0:T(2,128)(2,1)}, bf16[2,30,2,128]{3,2,1,0:T(2,128)(2,1)}, u32[]{:S(2)}, u32[]{:S(2)}) collective-permute-start(bf16[2,30,2,128]{3,2,1,0:T(2,128)(2,1)} %pad_maximum_fusion.13), channel_id=1, source_target_pairs={{0,4},{2,6},{4,8},{6,10},{8,12},{10,14},{12,16},{14,18},{16,20},{1... | collective-permute-start | bytes 92168 | tf_op jit(solution)/shard_map/ppermute | solution.py:16
  353.6 27.4 %collective-permute-start.22 = (bf16[2,30,2,128]{3,2,1,0:T(2,128)(2,1)}, bf16[2,30,2,128]{3,2,1,0:T(2,128)(2,1)}, u32[]{:S(2)}, u32[]{:S(2)}) collective-permute-start(bf16[2,30,2,128]{3,2,1,0:T(2,128)(2,1)} %pad_maximum_fusion.13), channel_id=1, source_target_pairs={{2,0},{4,2},{6,4},{8,6},{10,8},{12,10},{14,12},{16,14},{18,16},{20... | collective-permute-start | bytes 92168 | tf_op jit(solution)/shard_map/ppermute | solution.py:16
  367.0 14.1 %collective-permute-start.23 = (bf16[2,30,2,128]{3,2,1,0:T(2,128)(2,1)}, bf16[2,30,2,128]{3,2,1,0:T(2,128)(2,1)}, u32[]{:S(2)}, u32[]{:S(2)}) collective-permute-start(bf16[2,30,2,128]{3,2,1,0:T(2,128)(2,1)} %pad_maximum_fusion.13), channel_id=1, source_target_pairs={{0,2},{2,4},{4,6},{6,8},{8,10},{10,12},{12,14},{14,16},{16,18},{18... | collective-permute-start | bytes 92168 | tf_op jit(solution)/shard_map/ppermute | solution.py:16
  395.7 37.2 %copy-start.44 = (pred[128]{0:T(512)(128)(4,1)S(1)}, pred[128]{0:T(512)(128)(4,1)}, u32[]{:S(2)}) copy-start(pred[128]{0:T(512)(128)(4,1)} %copy-done.40) | copy-start | bytes 388
  397.7 35.7 %copy-start.39 = (pred[128]{0:T(512)(128)(4,1)S(1)}, pred[128]{0:T(512)(128)(4,1)}, u32[]{:S(2)}) copy-start(pred[128]{0:T(512)(128)(4,1)} %copy-done.35) | copy-start | bytes 388
  397.7 36.1 %copy-start.34 = (pred[128]{0:T(512)(128)(4,1)S(1)}, pred[128]{0:T(512)(128)(4,1)}, u32[]{:S(2)}) copy-start(pred[128]{0:T(512)(128)(4,1)} %copy-done.31) | copy-start | bytes 388
  399.0 35.3 %copy-start.30 = (pred[128]{0:T(512)(128)(4,1)S(1)}, pred[128]{0:T(512)(128)(4,1)}, u32[]{:S(2)}) copy-start(pred[128]{0:T(512)(128)(4,1)} %copy-done.27) | copy-start | bytes 388
  401.1 33.7 %copy-start.85 = (pred[128]{0:T(512)(128)(4,1)S(1)}, pred[128]{0:T(512)(128)(4,1)}, u32[]{:S(2)}) copy-start(pred[128]{0:T(512)(128)(4,1)} %select_compare_fusion.1) | copy-start | bytes 388
  401.4 33.4 %collective-permute-start.24 = (bf16[2,30,2,128]{3,2,1,0:T(2,128)(2,1)S(1)}, bf16[2,30,2,128]{3,2,1,0:T(2,128)(2,1)S(1)}, u32[]{:S(2)}, u32[]{:S(2)}) collective-permute-start(bf16[2,30,2,128]{3,2,1,0:T(2,128)(2,1)S(1)} %pad_maximum_fusion.14), channel_id=1, source_target_pairs={{4,0},{6,2},{8,4},{10,6},{12,8},{14,10},{16,12},{18,14},{20,16},{2... | collective-permute-start | bytes 92168 | tf_op jit(solution)/shard_map/ppermute | solution.py:16
  403.7 31.1 %collective-permute-start.25 = (bf16[2,30,2,128]{3,2,1,0:T(2,128)(2,1)S(1)}, bf16[2,30,2,128]{3,2,1,0:T(2,128)(2,1)S(1)}, u32[]{:S(2)}, u32[]{:S(2)}) collective-permute-start(bf16[2,30,2,128]{3,2,1,0:T(2,128)(2,1)S(1)} %pad_maximum_fusion.14), channel_id=1, source_target_pairs={{0,4},{2,6},{4,8},{6,10},{8,12},{10,14},{12,16},{14,18},{16,20},{1... | collective-permute-start | bytes 92168 | tf_op jit(solution)/shard_map/ppermute | solution.py:16
  407.3 27.5 %collective-permute-start.26 = (bf16[2,30,2,128]{3,2,1,0:T(2,128)(2,1)S(1)}, bf16[2,30,2,128]{3,2,1,0:T(2,128)(2,1)S(1)}, u32[]{:S(2)}, u32[]{:S(2)}) collective-permute-start(bf16[2,30,2,128]{3,2,1,0:T(2,128)(2,1)S(1)} %pad_maximum_fusion.14), channel_id=1, source_target_pairs={{2,0},{4,2},{6,4},{8,6},{10,8},{12,10},{14,12},{16,14},{18,16},{20... | collective-permute-start | bytes 92168 | tf_op jit(solution)/shard_map/ppermute | solution.py:16
  420.7 14.1 %collective-permute-start.27 = (bf16[2,30,2,128]{3,2,1,0:T(2,128)(2,1)S(1)}, bf16[2,30,2,128]{3,2,1,0:T(2,128)(2,1)S(1)}, u32[]{:S(2)}, u32[]{:S(2)}) collective-permute-start(bf16[2,30,2,128]{3,2,1,0:T(2,128)(2,1)S(1)} %pad_maximum_fusion.14), channel_id=1, source_target_pairs={{0,2},{2,4},{4,6},{6,8},{8,10},{10,12},{12,14},{14,16},{16,18},{18... | collective-permute-start | bytes 92168 | tf_op jit(solution)/shard_map/ppermute | solution.py:16
  452.2 33.7 %copy-start.83 = (pred[128]{0:T(512)(128)(4,1)S(1)}, pred[128]{0:T(512)(128)(4,1)}, u32[]{:S(2)}) copy-start(pred[128]{0:T(512)(128)(4,1)} %select_compare_fusion) | copy-start | bytes 388
  452.5 33.4 %collective-permute-start.28 = (bf16[2,30,2,128]{3,2,1,0:T(2,128)(2,1)S(1)}, bf16[2,30,2,128]{3,2,1,0:T(2,128)(2,1)S(1)}, u32[]{:S(2)}, u32[]{:S(2)}) collective-permute-start(bf16[2,30,2,128]{3,2,1,0:T(2,128)(2,1)S(1)} %pad_maximum_fusion.15), channel_id=1, source_target_pairs={{4,0},{6,2},{8,4},{10,6},{12,8},{14,10},{16,12},{18,14},{20,16},{2... | collective-permute-start | bytes 92168 | tf_op jit(solution)/shard_map/ppermute | solution.py:16
  454.9 31.1 %collective-permute-start.29 = (bf16[2,30,2,128]{3,2,1,0:T(2,128)(2,1)S(1)}, bf16[2,30,2,128]{3,2,1,0:T(2,128)(2,1)S(1)}, u32[]{:S(2)}, u32[]{:S(2)}) collective-permute-start(bf16[2,30,2,128]{3,2,1,0:T(2,128)(2,1)S(1)} %pad_maximum_fusion.15), channel_id=1, source_target_pairs={{0,4},{2,6},{4,8},{6,10},{8,12},{10,14},{12,16},{14,18},{16,20},{1... | collective-permute-start | bytes 92168 | tf_op jit(solution)/shard_map/ppermute | solution.py:16
  458.4 27.5 %collective-permute-start.30 = (bf16[2,30,2,128]{3,2,1,0:T(2,128)(2,1)S(1)}, bf16[2,30,2,128]{3,2,1,0:T(2,128)(2,1)S(1)}, u32[]{:S(2)}, u32[]{:S(2)}) collective-permute-start(bf16[2,30,2,128]{3,2,1,0:T(2,128)(2,1)S(1)} %pad_maximum_fusion.15), channel_id=1, source_target_pairs={{2,0},{4,2},{6,4},{8,6},{10,8},{12,10},{14,12},{16,14},{18,16},{20... | collective-permute-start | bytes 92168 | tf_op jit(solution)/shard_map/ppermute | solution.py:16
  471.8 14.1 %collective-permute-start.31 = (bf16[2,30,2,128]{3,2,1,0:T(2,128)(2,1)S(1)}, bf16[2,30,2,128]{3,2,1,0:T(2,128)(2,1)S(1)}, u32[]{:S(2)}, u32[]{:S(2)}) collective-permute-start(bf16[2,30,2,128]{3,2,1,0:T(2,128)(2,1)S(1)} %pad_maximum_fusion.15), channel_id=1, source_target_pairs={{0,2},{2,4},{4,6},{6,8},{8,10},{10,12},{12,14},{14,16},{16,18},{18... | collective-permute-start | bytes 92168 | tf_op jit(solution)/shard_map/ppermute | solution.py:16
  (68 other events, 513.5 us)
where the time goes:
time: 510 us; the launch traced here: 501 us
  starting transfers between devices  172 us (34%)
  matrix products  129 us (25%)
  local copies, waits for them, and re-layouts  110 us (22%)
  other arithmetic  44.1 us (9%)
  blocking collectives  41.2 us (8%)
  between operations  5.95 us (1%)
    ppermute x32, starting transfers between devices, from_behind(): lax.ppermute(value, axis, [(source, source + steps) for source in range(i...  172 us
    all_gather x7, blocking collectives, gather_fields(): return lax.all_gather(values, 'blk', axis=3, tiled=True)  41.2 us
    gather x32, local copies, waits for them, and re-layouts, solve_layout(): nearby = jnp.take(padded, neighbours[:, face_no], axis=3)  37 us
    dot_general x8, matrix products, solve_layout(): jnp.einsum('ije,jse->ise', inverse[1], right_side[1], preferred_element_t...  32.2 us
    dot_general x8, matrix products, solve_layout(): jnp.einsum('ije,jse->ise', inverse[1], right_side[0], preferred_element_t...  31.1 us
    unnamed x202, local copies, waits for them, and re-layouts  22.2 us
    gather x4, local copies, waits for them, and re-layouts, solve_layout(): chosen = jnp.take(trace_matrices, slot_codes % 4, axis=0)  17.4 us
    dot_general x8, matrix products, solve_layout(): jnp.einsum('ije,jse->ise', inverse[0], right_side[0], preferred_element_t...  16.2 us
  transfers between devices with their start and end apart: 32, of which 0 were waited for; matrix products, arithmetic and copies ran while one was open for 25% of the time, Pallas kernels for 0%

commit v1 on v0

v1 whole, which is shorter than its diff:
```python
import functools

import jax
import jax.numpy as jnp
from jax import lax
from jax.experimental import pallas as pl
from jax.experimental.pallas import tpu as pltpu
from jax.sharding import PartitionSpec as P

BF = jnp.bfloat16
F32 = jnp.float32
I32 = jnp.int32
DOF = 105
TDOF = 30
E_DEV = 128
ITERS = 2
ROUNDS = 4
STEPS = ITERS * ROUNDS
L = 128
JP = 112
SHIFTS = (1, -1, 2, -2)
NT = (((1,), (1,)), ((), ()))


def dot(a, b):
    return jnp.dot(a, b, preferred_element_type=F32)


def dot_nt(a, b):
    return lax.dot_general(a, b, NT, preferred_element_type=F32)


def iota(shape, axis):
    return lax.broadcasted_iota(I32, shape, axis)


def hot(mask):
    return jnp.where(mask, 1.0, 0.0).astype(BF)


def row(ref, *index):
    return ref[index[:-1] + (pl.ds(index[-1], 1), slice(None))]


def kernel(
    n_sub,
    inverse,
    source,
    face_t,
    trace_t,
    trace_n,
    neighbours,
    coupling,
    slots,
    robin,
    matching,
    counts,
    out,
    packed,
    tail,
    wide,
    staged,
    weights,
    eye,
    near,
    pick,
    lift_hot,
    to_trace,
    from_trace,
    robin_re,
    robin_im,
    couple,
    base,
    lifted,
    interface,
    rhs,
    left,
    product,
    field,
    far_field,
    outgoing,
    arriving,
    load_sem,
    field_send,
    field_recv,
    robin_send,
    robin_recv,
):
    sub = lax.axis_index("sub")
    blk = lax.axis_index("blk")
    loads = inverse.reshape(DOF, 2 * DOF, L)
    load_main = pltpu.make_async_copy(loads.at[:, pl.ds(0, 208)], packed, load_sem.at[0])
    load_tail = pltpu.make_async_copy(loads.at[:, pl.ds(208, 2)], tail, load_sem.at[1])
    load_main.start()
    load_tail.start()
    arriving[...] = jnp.zeros_like(arriving)

    barrier = pltpu.get_barrier_semaphore()
    for shift in SHIFTS:

        @pl.when((sub + shift >= 0) & (sub + shift < n_sub))
        def _(shift=shift):
            pl.semaphore_signal(
                barrier,
                inc=1,
                device_id=(sub + shift, blk),
                device_id_type=pl.DeviceIdType.MESH,
            )

    pl.semaphore_signal(
        barrier, inc=1, device_id=(sub, 1 - blk), device_id_type=pl.DeviceIdType.MESH
    )

    square = (L, L)
    rows, lanes = iota(square, 0), iota(square, 1)
    eye[...] = hot(rows == lanes)
    identity = eye[...]
    for f in range(4):
        code = jnp.broadcast_to(row(neighbours, f), square)
        mine = hot(code == rows + blk * E_DEV)
        theirs = hot(code == rows + (1 - blk) * E_DEV)
        near[pl.ds(f * L, L), 0:L] = dot_nt(identity, mine).astype(BF)
        near[pl.ds(f * L, L), L : 2 * L] = dot_nt(identity, theirs).astype(BF)
        for c in range(2):
            value = jnp.broadcast_to(row(coupling, f, c), square)
            couple[f, c] = dot_nt(identity, value)
    sign = jnp.where((lanes // 32) % 2 == 0, -2.0, 2.0)
    for r in range(ROUNDS):
        code = jnp.broadcast_to(row(slots, r), square)
        live = lanes < counts[r, 0]
        for f in range(4):
            mask = code == 4 * rows + f
            pick[r, :, pl.ds(f * L, L)] = dot_nt(identity, hot(mask)).astype(BF)
            lift_hot[r, pl.ds(f * L, L), :] = hot(mask & live)
        robin_re[r] = 2.0 * dot_nt(identity, jnp.broadcast_to(row(robin, 0, r), square))
        robin_im[r] = sign * dot_nt(identity, jnp.broadcast_to(row(robin, 1, r), square))
        lifted[r] = jnp.zeros((E_DEV, 4 * L), F32)
        interface[r] = jnp.zeros(square, BF)
    wide_shape = (L, 4 * L)
    fk, lane = iota(wide_shape, 0), iota(wide_shape, 1)
    tall_shape = (4 * L, L)
    trow, tfk = iota(tall_shape, 0), iota(tall_shape, 1)
    for part in range(4):
        spread = hot((lane // L == fk // 32) & (lane % L == part * 32 + fk % 32))
        to_trace[pl.ds(part * L, L), :] = dot(trace_t[...], spread).astype(BF)
        spread = hot((trow // L == tfk // 32) & (trow % L == part * 32 + tfk % 32))
        from_trace[:, pl.ds(part * L, L)] = dot(spread, trace_n[...]).astype(BF)
    base[...] = source[...].astype(F32)
    left[...] = jnp.zeros_like(left)
    rhs[...] = base[...]

    load_main.wait()
    load_tail.wait()

    def widen(i, carry):
        start = pl.multiple_of(i * 224, 8)
        wide[pl.ds(start, 208), :] = packed[i].astype(F32)
        last = tail[i].astype(F32)
        wide[pl.ds(pl.multiple_of(start + 208, 8), 16), :] = jnp.concatenate(
            [last, jnp.zeros((14, L), F32)], axis=0
        )
        return carry

    lax.fori_loop(0, DOF, widen, 0)

    def blank(i, carry):
        wide[pl.ds(pl.multiple_of(i * 224, 8), 224), :] = jnp.zeros((224, L), F32)
        return carry

    lax.fori_loop(DOF, JP, blank, 0)

    def clear(e, carry):
        weights[e, JP:L, :] = jnp.zeros((L - JP, 2 * L), BF)
        return carry

    lax.fori_loop(0, E_DEV, clear, 0)

    def regroup(group, carry):
        for inner in range(16):
            for c in range(2):
                block = wide[pl.ds(group * 32 + 2 * inner + c, JP, stride=224), :]
                block = jnp.concatenate([block, jnp.zeros((L - JP, L), F32)], axis=0).astype(BF)
                staged[c, pl.ds(inner, E_DEV, stride=16), :] = dot_nt(identity, block)

        def pack(chunk, inner_carry):
            for q in range(8):
                e = chunk * 8 + q
                for c in range(2):
                    tile = staged[c, pl.ds(pl.multiple_of(e * 16, 16), 16), :].astype(BF)
                    weights[e, pl.ds(pl.multiple_of(group * 16, 16), 16), c * L : (c + 1) * L] = tile
            return inner_carry

        lax.fori_loop(0, E_DEV // 8, pack, 0)
        return carry

    lax.fori_loop(0, JP // 16, regroup, 0)

    neighbours_there = jnp.int32(1)
    for shift in SHIFTS:
        there = (sub + shift >= 0) & (sub + shift < n_sub)
        neighbours_there = neighbours_there + there.astype(I32)
    pl.semaphore_wait(barrier, neighbours_there)

    def field_copy(slot):
        return pltpu.make_async_remote_copy(
            src_ref=field.at[slot],
            dst_ref=far_field.at[slot],
            send_sem=field_send.at[slot],
            recv_sem=field_recv.at[slot],
            device_id=(sub, 1 - blk),
            device_id_type=pl.DeviceIdType.MESH,
        )

    def robin_copy(slot, which):
        return pltpu.make_async_remote_copy(
            src_ref=outgoing.at[slot],
            dst_ref=arriving.at[slot, which],
            send_sem=robin_send.at[slot, which],
            recv_sem=robin_recv.at[slot, which],
            device_id=(sub + SHIFTS[which], blk),
            device_id_type=pl.DeviceIdType.MESH,
        )

    def exchange(step):
        slot = lax.rem(step, 2)
        r = lax.rem(step, ROUNDS)
        own = field[slot]
        spread = dot(own, to_trace[...]).astype(BF)
        stacked = jnp.concatenate([spread[:, f * L : (f + 1) * L] for f in range(4)], axis=0)
        traced = dot(pick[r], stacked)
        turned = jnp.where(
            (lanes // 32) % 2 == 0, pltpu.roll(traced, L - 32, 1), pltpu.roll(traced, 32, 1)
        )
        former = interface[r]
        sent = robin_re[r] * traced + robin_im[r] * turned - former.astype(F32)
        outgoing[slot] = sent.astype(BF)
        for which, shift in enumerate(SHIFTS):

            @pl.when((sub + shift >= 0) & (sub + shift < n_sub))
            def _(which=which):
                robin_copy(slot, which).start()

        field_copy(slot).wait_recv()
        both = jnp.concatenate([own, far_field[slot]], axis=0)
        total = [base[:, p * L : (p + 1) * L] for p in range(4)]
        for f in range(4):
            gathered = dot(near[pl.ds(f * L, L), :], both).astype(BF)
            flux = [dot(gathered[:, p * L : (p + 1) * L], face_t[f]) for p in range(4)]
            re, im = couple[f, 0], couple[f, 1]
            for s in range(2):
                total[2 * s] += re * flux[2 * s] - im * flux[2 * s + 1]
                total[2 * s + 1] += re * flux[2 * s + 1] + im * flux[2 * s]
        for p in range(4):
            rhs[:, p * L : (p + 1) * L] = total[p]

        for which, shift in enumerate(SHIFTS):

            @pl.when((sub - shift >= 0) & (sub - shift < n_sub))
            def _(which=which):
                robin_copy(slot, which).wait_recv()

        offset = jnp.broadcast_to(matching[r, 0] - sub, square)
        arrived = jnp.zeros(square, BF).astype(F32)
        for which, shift in enumerate(SHIFTS):
            arrived = jnp.where(offset == -shift, arriving[slot, which].astype(F32), arrived)
        live = rows < counts[r, 0]
        updated = jnp.where(live, arrived, former.astype(F32)).astype(BF)
        interface[r] = updated
        landed = dot(lift_hot[r], updated).astype(BF)
        side = jnp.concatenate([landed[f * L : (f + 1) * L] for f in range(4)], axis=1)
        lifted[r] = dot(side, from_trace[...])
        rhs[...] += lifted[0] + lifted[1] + lifted[2] + lifted[3]

        field_copy(slot).wait_send()
        for which, shift in enumerate(SHIFTS):

            @pl.when((sub + shift >= 0) & (sub + shift < n_sub))
            def _(which=which):
                robin_copy(slot, which).wait_send()

    half = E_DEV // 2

    def advance(step, carry):
        pl.when(step > 0)(lambda: exchange(step))
        following = lax.rem(step + 1, 2)
        for el in range(2):
            for c in range(2):
                for s in range(2):
                    p = 2 * s + c
                    left[el, pl.ds(el * 4 + c * 2 + s, half, stride=8), :] = rhs[
                        el * half : (el + 1) * half, p * L : (p + 1) * L
                    ]

        def solve(chunk, inner):
            for q in range(16):
                pair = chunk * 16 + q
                spot = pl.ds(pl.multiple_of(pair * 8, 8), 8)
                vector = jnp.concatenate([left[0, spot, :], left[1, spot, :]], axis=1).astype(BF)
                matrix = jnp.concatenate([weights[pair], weights[half + pair]], axis=0)
                result = dot(vector, matrix)
                product[0, spot, :] = result[:, 0:L]
                product[1, spot, :] = result[:, L : 2 * L]
            return inner

        lax.fori_loop(0, half // 16, solve, 0)
        for el in range(2):
            for s in range(2):
                at = [pl.ds(el * 4 + c * 2 + s, half, stride=8) for c in range(2)]
                re = product[0, at[0], :] - product[1, at[1], :]
                im = product[1, at[0], :] + product[0, at[1], :]
                field[following, el * half : (el + 1) * half, 2 * s * L : (2 * s + 1) * L] = (
                    re.astype(BF)
                )
                field[following, el * half : (el + 1) * half, (2 * s + 1) * L : (2 * s + 2) * L] = (
                    im.astype(BF)
                )

        @pl.when(step < STEPS - 1)
        def _():
            field_copy(following).start()

        return carry

    lax.fori_loop(0, STEPS, advance, 0)
    final = STEPS % 2
    for s in range(2):
        for c in range(2):
            p = 2 * s + c
            out[2 * c + s] = dot_nt(identity, field[final, :, p * L : (p + 1) * L]).astype(BF)


def shards(
    n_sub,
    source_terms,
    inverse_blocks,
    face_matrices,
    trace_matrices,
    neighbours,
    coupling,
    slot_faces,
    robin_params,
    matching,
    counts,
):
    inverse = jnp.transpose(inverse_blocks, (1, 2, 0, 3))
    source = jnp.pad(
        jnp.transpose(source_terms, (3, 2, 0, 1)), ((0, 0), (0, 0), (0, 0), (0, L - DOF))
    ).reshape(E_DEV, 4 * L)
    grow = L - DOF
    face_t = jnp.pad(jnp.transpose(face_matrices, (0, 2, 1)), ((0, 0), (0, grow), (0, grow)))
    trace_n = jnp.pad(trace_matrices, ((0, 0), (0, 32 - TDOF), (0, grow))).reshape(L, L)
    trace_t = jnp.transpose(trace_n)
    vmem = pl.BlockSpec(memory_space=pltpu.VMEM)
    smem = pl.BlockSpec(memory_space=pltpu.SMEM)
    square = (L, L)
    result = pl.pallas_call(
        functools.partial(kernel, n_sub),
        out_shape=jax.ShapeDtypeStruct((4, L, E_DEV), BF),
        in_specs=[pl.BlockSpec(memory_space=pl.ANY)] + [vmem] * 8 + [smem] * 2,
        out_specs=vmem,
        scratch_shapes=[
            pltpu.VMEM((DOF, 208, L), BF),
            pltpu.VMEM((DOF, 2, L), BF),
            pltpu.VMEM((JP * 224, L), F32),
            pltpu.VMEM((2, 16 * E_DEV, L), F32),
            pltpu.VMEM((E_DEV, L, 2 * L), BF),
            pltpu.VMEM(square, BF),
            pltpu.VMEM((4 * L, 2 * L), BF),
            pltpu.VMEM((ROUNDS, L, 4 * L), BF),
            pltpu.VMEM((ROUNDS, 4 * L, L), BF),
            pltpu.VMEM((4 * L, 4 * L), BF),
            pltpu.VMEM((4 * L, 4 * L), BF),
            pltpu.VMEM((ROUNDS, L, L), F32),
            pltpu.VMEM((ROUNDS, L, L), F32),
            pltpu.VMEM((4, 2, L, L), F32),
            pltpu.VMEM((E_DEV, 4 * L), F32),
            pltpu.VMEM((ROUNDS, E_DEV, 4 * L), F32),
            pltpu.VMEM((ROUNDS, L, L), BF),
            pltpu.VMEM((E_DEV, 4 * L), F32),
            pltpu.VMEM((2, 4 * E_DEV, L), F32),
            pltpu.VMEM((2, 4 * E_DEV, L), F32),
            pltpu.VMEM((2, E_DEV, 4 * L), BF),
            pltpu.VMEM((2, E_DEV, 4 * L), BF),
            pltpu.VMEM((2, L, L), BF),
            pltpu.VMEM((2, 4, L, L), BF),
            pltpu.SemaphoreType.DMA((2,)),
            pltpu.SemaphoreType.DMA((2,)),
            pltpu.SemaphoreType.DMA((2,)),
            pltpu.SemaphoreType.DMA((2, 4)),
            pltpu.SemaphoreType.DMA((2, 4)),
        ],
        compiler_params=pltpu.CompilerParams(
            collective_id=0, has_side_effects=True, vmem_limit_bytes=56 * 2**20
        ),
    )(
        inverse,
        source,
        face_t,
        trace_t,
        trace_n,
        jnp.transpose(neighbours),
        jnp.transpose(coupling, (1, 2, 0)),
        slot_faces[0],
        robin_params[:, 0],
        matching,
        counts[:, :, 0],
    )
    return result.reshape(2, 2, L, E_DEV)[:, :, :DOF].transpose(0, 2, 1, 3)


def solution(mesh):
    in_specs = (
        P(None, None, None, ("sub", "blk")),
        P(None, None, None, ("sub", "blk")),
        P(),
        P(),
        P(("sub", "blk"), None),
        P(("sub", "blk"), None, None),
        P("sub", None, "blk"),
        P(None, "sub", None, "blk"),
        P(None, "sub"),
        P(None, "sub", "blk"),
    )
    out_specs = P(None, None, None, ("sub", "blk"))
    body = functools.partial(shards, mesh.shape["sub"])
    return jax.shard_map(body, mesh=mesh, in_specs=in_specs, out_specs=out_specs, check_vma=False)
```

time: 510 us -> 100 us (0.20); the launches traced: 501 us -> 100 us
  starting transfers between devices: 172 us -> 0 us
  matrix products: 129 us -> 0 us
  local copies, waits for them, and re-layouts: 110 us -> 9.38 us
  Pallas kernels: 0 us -> 90.6 us
  other arithmetic: 44.1 us -> 0 us
  blocking collectives: 41.2 us -> 0 us
  between operations: 5.95 us -> 0.04 us
    ppermute x32 -> x0, starting transfers between devices: 172 us -> none  [from_behind(): lax.ppermute(value, axis, [(source, source + steps) for source in range(i...]
    dot_general x88 -> x0, matrix products: 129 us -> none  [the longest x8 32.2 us: solve_layout(): jnp.einsum('ije,jse->ise', inverse[1], right_side[1], preferred_element_t...]
    pallas_call x0 -> x1, Pallas kernels: none -> 90.6 us  [shards(): pl.pallas_call(functools.partial(kernel, n_sub), out_shape=jax.ShapeDtype...]
    gather x44 -> x0, local copies, waits for them, and re-layouts: 62.5 us -> none  [the longest x32 37 us: solve_layout(): nearby = jnp.take(padded, neighbours[:, face_no], axis=3)]
    all_gather x7 -> x0, blocking collectives: 41.2 us -> none  [gather_fields(): return lax.all_gather(values, 'blk', axis=3, tiled=True)]
    select_n x41 -> x0, other arithmetic: 20.2 us -> none  [the longest x30 14.2 us: solve_layout(): nearby = jnp.take(padded, neighbours[:, face_no], axis=3)]
    unnamed x202 -> x7, local copies, waits for them, and re-layouts: 22.2 us -> 4.89 us
    slice x4 -> x1, local copies, waits for them, and re-layouts: 15.2 us -> 0.91 us  [shards(): return result.reshape(2, 2, L, E_DEV)[:, :, :DOF].transpose(0, 2, 1, 3)]
  transfers between devices with their start and end apart: 32 -> 0, of which waited for: 0 -> 0; matrix products, arithmetic and copies ran while one was open for 25% -> 0% of each run, Pallas kernels for 0% -> 0%
where the time goes in v1:
time: 100 us
  Pallas kernels  90.6 us (91%)
  local copies, waits for them, and re-layouts  9.38 us (9%)
    pallas_call x1, Pallas kernels, shards(): pl.pallas_call(functools.partial(kernel, n_sub), out_shape=jax.ShapeDtype...  90.6 us
    unnamed x7, local copies, waits for them, and re-layouts  4.89 us

profile of v1, /device:TPU:6, one launch (start us, length us, event | category | flops | bytes accessed | tf_op | source)
XLA Modules:
  0.0 100.0 jit_solution(11225700605597522338)
XLA Ops:
  0.0 1.3 %copy.15.matching = s32[4,1]{1,0:T(4,128)} copy(s32[4,1]{0,1:T(1,128)} %param.18) | data formatting | bytes 32 | tf_op args[8]
  1.3 1.3 %copy.16.counts = s32[4,1]{1,0:T(4,128)} copy(s32[4,1]{0,1:T(1,128)} %bitcast.25) | data formatting | bytes 32 | tf_op jit(solution)/shard_map/squeeze | solution.py:406
  2.6 0.8 copy.20
  3.4 0.0 copy-start
  3.4 0.7 copy.14.trace_t
  4.1 1.1 %copy.12 = bf16[4,105,105]{1,2,0:T(8,128)(2,1)S(1)} copy(bf16[4,105,105]{2,0,1:T(4,128)(2,1)} %param.12) | data formatting | bytes 176400 | tf_op args[2]
  5.2 0.7 pad.13.face_t
  5.9 1.0 %copy.19 = bf16[128,2,2,105]{3,2,1,0:T(2,128)(2,1)S(1)} copy(bf16[128,2,2,105]{0,1,3,2:T(2,128)(2,1)} %bitcast.20) | data formatting | bytes 215040
  6.9 0.1 pad.12.clone
  7.1 0.7 reshape.9.source
  7.8 0.0 copy-done
  7.8 90.6 %shard_map.100 = bf16[4,128,128]{2,1,0:T(8,128)(2,1)} custom-call(bf16[105,105,2,128]{3,2,1,0:T(2,128)(2,1)} %bitcast.15, bf16[128,512]{1,0:T(8,128)(2,1)} %reshape.9.source, bf16[4,128,128]{2,1,0:T(8,128)(2,1)} %pad.13.face_t, bf16[128,128]{1,0:T(8,128)(2,1)} %copy.14.trace_t, bf16[128,128]{1,0:T(8,128)(2,1)} %bitcast.19, s32[4,128]{1,0:T(4,128)} %bitcast.21, ...), custom_call_target="tpu_custom_call" | custom-call | tf_op jit(solution)/shard_map/pallas_call | solution.py:356
  98.4 0.9 slice.4
  99.3 0.7 copy.22
  (1 shorter events, 0.0 us)
Async XLA Ops:
  3.4 4.4 %copy-start = (bf16[4,32,128]{2,1,0:T(8,128)(2,1)}, bf16[4,32,128]{2,1,0:T(8,128)(2,1)S(1)}, u32[]{:S(2)}) copy-start(bf16[4,32,128]{2,1,0:T(8,128)(2,1)S(1)} %pad.14.clone) | copy-start | bytes 98308

commit v2 on v1

v2 whole, which is shorter than its diff:
```python
import functools

import jax
import jax.numpy as jnp
from jax import lax
from jax.experimental import pallas as pl
from jax.experimental.pallas import tpu as pltpu
from jax.sharding import PartitionSpec as P

BF = jnp.bfloat16
F32 = jnp.float32
I32 = jnp.int32
DOF = 105
TDOF = 30
E_DEV = 128
ITERS = 2
ROUNDS = 4
STEPS = ITERS * ROUNDS
L = 128
JP = 112
PITCH = 216
PARTS = 3
SHIFTS = (1, -1, 2, -2)
NT = (((1,), (1,)), ((), ()))


def dot(a, b):
    return jnp.dot(a, b, preferred_element_type=F32)


def dot_nt(a, b):
    return lax.dot_general(a, b, NT, preferred_element_type=F32)


def iota(shape, axis):
    return lax.broadcasted_iota(I32, shape, axis)


def hot(mask):
    return jnp.where(mask, 1.0, 0.0).astype(BF)


def row(ref, *index):
    return ref[index[:-1] + (pl.ds(index[-1], 1), slice(None))]


def kernel(
    n_sub,
    inverse,
    source,
    face,
    trace,
    neighbours_in,
    coupling_in,
    slots_in,
    robin_in,
    matching_in,
    counts_in,
    out,
    packed,
    tail,
    source_rows,
    source_tail,
    source_wide,
    face_rows,
    face_tail,
    trace_rows,
    trace_tail,
    face_t,
    neighbours,
    coupling,
    slots,
    robin,
    matching,
    counts,
    wide,
    staged,
    weights,
    eye,
    near,
    pick,
    lift_hot,
    to_trace,
    from_trace,
    robin_re,
    robin_im,
    couple,
    base,
    lifted,
    interface,
    rhs,
    left,
    product,
    field,
    far_field,
    outgoing,
    arriving,
    trace_n_ref,
    eye_wide,
    load_sem,
    field_send,
    field_recv,
    robin_send,
    robin_recv,
):
    sub = lax.axis_index("sub")
    blk = lax.axis_index("blk")
    trace_flat = trace.reshape(4 * TDOF, DOF)
    source_flat = source.reshape(2, 2 * DOF, L)
    face_flat = face.reshape(4 * DOF, DOF)
    loads = inverse.reshape(DOF, 2 * DOF, L)
    small = [
        (slots_in, slots),
        (robin_in, robin),
        (neighbours_in, neighbours),
        (coupling_in, coupling),
        (matching_in, matching),
        (counts_in, counts),
    ]
    moves = [
        (trace_flat.at[pl.ds(0, 112)], trace_rows.at[pl.ds(0, 112)]),
        (trace.at[pl.ds(28, 2)], trace_tail),
        (source_flat.at[:, pl.ds(0, 208)], source_rows),
        (source_flat.at[:, pl.ds(208, 2)], source_tail),
        (loads.at[:, pl.ds(208, 2)], tail),
    ]
    for part in range(PARTS):
        chunk = pl.ds(part * (DOF // PARTS), DOF // PARTS)
        moves.append((loads.at[chunk, pl.ds(0, 208)], packed.at[chunk]))
    moves.append((face_flat.at[pl.ds(0, 416)], face_rows.at[pl.ds(0, 416)]))
    moves.append((face.at[DOF - 1], face_tail))
    moves += small
    moves = [pltpu.make_async_copy(a, b, load_sem.at[n]) for n, (a, b) in enumerate(moves)]
    for move in moves:
        move.start()
    arriving[...] = jnp.zeros_like(arriving)

    barrier = pltpu.get_barrier_semaphore()
    for shift in SHIFTS:

        @pl.when((sub + shift >= 0) & (sub + shift < n_sub))
        def _(shift=shift):
            pl.semaphore_signal(
                barrier,
                inc=1,
                device_id=(sub + shift, blk),
                device_id_type=pl.DeviceIdType.MESH,
            )

    pl.semaphore_signal(
        barrier, inc=1, device_id=(sub, 1 - blk), device_id_type=pl.DeviceIdType.MESH
    )

    square = (L, L)
    rows, lanes = iota(square, 0), iota(square, 1)
    eye[...] = hot(rows == lanes)
    identity = eye[...]
    eye_wide[...] = hot(iota((2 * L, 2 * L), 0) == iota((2 * L, 2 * L), 1))
    left[...] = jnp.zeros_like(left)
    lifted[...] = jnp.zeros_like(lifted)
    interface[...] = jnp.zeros_like(interface)

    first_small = 7 + PARTS
    for n in range(2):
        moves[first_small + n].wait()
    sign = jnp.where((lanes // 32) % 2 == 0, -2.0, 2.0)
    for r in range(ROUNDS):
        code = jnp.broadcast_to(row(slots, r), square)
        for f in range(4):
            pick[r, :, pl.ds(f * L, L)] = dot_nt(identity, hot(code == 4 * rows + f)).astype(BF)
        robin_re[r] = 2.0 * dot_nt(identity, jnp.broadcast_to(row(robin, 0, r), square))
        robin_im[r] = sign * dot_nt(identity, jnp.broadcast_to(row(robin, 1, r), square))
    moves[0].wait()
    moves[1].wait()
    last = trace_tail[...].astype(F32).reshape(8, DOF)
    trace_rows[112:128, :] = jnp.concatenate([last, jnp.zeros((8, DOF), F32)], axis=0).astype(BF)
    trace_n = dot(trace_rows[...], eye[0:DOF, :]).astype(BF)
    trace_t = dot_nt(identity, trace_n).astype(BF)
    wide_shape = (L, 4 * L)
    kf, lane = iota(wide_shape, 0), iota(wide_shape, 1)
    for part in range(4):
        spread = hot((lane // L == kf % 4) & (lane % L == part * 32 + kf // 4))
        to_trace[pl.ds(part * L, L), :] = dot(trace_t, spread).astype(BF)

    moves[2].wait()
    moves[3].wait()
    for c in range(2):
        source_wide[pl.ds(c * 256, 208), :] = source_rows[c].astype(F32)
        source_wide[pl.ds(c * 256 + 208, 48), :] = jnp.concatenate(
            [source_tail[c].astype(F32), jnp.zeros((46, L), F32)], axis=0
        )
    for s in range(2):
        for c in range(2):
            p = 2 * s + c
            block = source_wide[pl.ds(c * 256 + s, L, stride=2), :].astype(BF)
            base[:, p * L : (p + 1) * L] = dot_nt(identity, block)

    def rest_of_constants():
        for f in range(4):
            code = jnp.broadcast_to(row(neighbours, f), square)
            mine = hot(code == rows + blk * E_DEV)
            theirs = hot(code == rows + (1 - blk) * E_DEV)
            near[pl.ds(f * L, L), 0:L] = dot_nt(identity, mine).astype(BF)
            near[pl.ds(f * L, L), L : 2 * L] = dot_nt(identity, theirs).astype(BF)
            for c in range(2):
                value = jnp.broadcast_to(row(coupling, f, c), square)
                couple[f, c] = dot_nt(identity, value)
        for r in range(ROUNDS):
            code = jnp.broadcast_to(row(slots, r), square)
            live = lanes < counts[0, r]
            for f in range(4):
                lift_hot[r, pl.ds(f * L, L), :] = hot((code == 4 * rows + f) & live)
        trow, tkf = iota((4 * L, L), 0), iota((4 * L, L), 1)
        for part in range(4):
            spread = hot((trow // L == tkf % 4) & (trow % L == part * 32 + tkf // 4))
            from_trace[:, pl.ds(part * L, L)] = dot(spread, trace_n_ref[...]).astype(BF)
        end = jnp.concatenate([face_tail[...].astype(F32), jnp.zeros((12, DOF), F32)], axis=0)
        face_rows[416:432, :] = end.astype(BF)
        frow, fk = iota((L, 432), 0), iota((L, 432), 1)
        for f in range(4):
            chosen = dot(hot(4 * frow + f == fk), face_rows[...]).astype(BF)
            face_t[f] = dot_nt(eye[:, 0:DOF], chosen).astype(BF)

    trace_n_ref[...] = trace_n

    def clear(e, carry):
        for q in range(8):
            weights[e * 8 + q, JP:L, :] = jnp.zeros((L - JP, 2 * L), BF)
        return carry

    lax.fori_loop(0, E_DEV // 8, clear, 0)
    rest = (JP - DOF) * PITCH + 8
    wide[pl.ds(DOF * PITCH, rest), :] = jnp.zeros((rest, L), F32)
    moves[4].wait()

    def widen(chunk, carry):
        for q in range(5):
            i = chunk * 5 + q
            start = pl.multiple_of(i * PITCH, 8)
            wide[pl.ds(start, 208), :] = packed[i].astype(F32)
            wide[pl.ds(pl.multiple_of(start + 208, 8), 8), :] = jnp.concatenate(
                [tail[i].astype(F32), jnp.zeros((6, L), F32)], axis=0
            )
        return carry

    each = DOF // PARTS // 5
    for part in range(PARTS):
        moves[5 + part].wait()
        lax.fori_loop(part * each, (part + 1) * each, widen, 0)
    for n in range(5 + PARTS, 7 + PARTS + len(small)):
        if n not in (first_small, first_small + 1):
            moves[n].wait()

    def regroup(group, carry):
        def block(inner, c):
            value = wide[pl.ds(group * 32 + 2 * inner + c, JP, stride=PITCH), :]
            return jnp.concatenate([value, jnp.zeros((L - JP, L), F32)], axis=0)

        for pair in range(8):
            inners = (2 * pair, 2 * pair + 1)
            if pair in (0, 2, 4, 5, 7):
                both = [
                    jnp.concatenate([block(n, 0), block(n, 1)], axis=0).astype(BF) for n in inners
                ]
                result = dot_nt(eye_wide[...], jnp.concatenate(both, axis=1))
                turned = [
                    [result[n * L : (n + 1) * L, c * L : (c + 1) * L] for c in range(2)]
                    for n in range(2)
                ]
            else:
                turned = [[block(n, c).T for c in range(2)] for n in inners]
            for n, inner in enumerate(inners):
                for c in range(2):
                    staged[c, inner // 8, pl.ds(inner % 8, E_DEV, stride=8), :] = turned[n][c]

        def pack(chunk, inner_carry):
            for q in range(16):
                e = chunk * 16 + q
                spot = pl.ds(pl.multiple_of(e * 8, 8), 8)
                for c in range(2):
                    tile = jnp.concatenate([staged[c, 0, spot, :], staged[c, 1, spot, :]], axis=0)
                    weights[e, pl.ds(pl.multiple_of(group * 16, 16), 16), c * L : (c + 1) * L] = (
                        tile.astype(BF)
                    )
            return inner_carry

        lax.fori_loop(0, E_DEV // 16, pack, 0)
        return carry

    lax.fori_loop(0, JP // 16, regroup, 0)

    neighbours_there = jnp.int32(1)
    for shift in SHIFTS:
        there = (sub + shift >= 0) & (sub + shift < n_sub)
        neighbours_there = neighbours_there + there.astype(I32)
    pl.semaphore_wait(barrier, neighbours_there)

    half = E_DEV // 2

    def field_copy(slot):
        return pltpu.make_async_remote_copy(
            src_ref=field.at[slot],
            dst_ref=far_field.at[slot],
            send_sem=field_send.at[slot],
            recv_sem=field_recv.at[slot],
            device_id=(sub, 1 - blk),
            device_id_type=pl.DeviceIdType.MESH,
        )

    def robin_copy(slot, which):
        return pltpu.make_async_remote_copy(
            src_ref=outgoing.at[slot],
            dst_ref=arriving.at[slot, which],
            send_sem=robin_send.at[slot, which],
            recv_sem=robin_recv.at[slot, which],
            device_id=(sub + SHIFTS[which], blk),
            device_id_type=pl.DeviceIdType.MESH,
        )

    def exchange(step):
        slot = lax.rem(step, 2)
        r = lax.rem(step, ROUNDS)
        own = field[slot]
        spread = dot(own, to_trace[...]).astype(BF)
        stacked = jnp.concatenate([spread[:, f * L : (f + 1) * L] for f in range(4)], axis=0)
        traced = dot(pick[r], stacked)
        turned = jnp.where(
            (lanes // 32) % 2 == 0, pltpu.roll(traced, L - 32, 1), pltpu.roll(traced, 32, 1)
        )
        former = interface[r]
        sent = robin_re[r] * traced + robin_im[r] * turned - former.astype(F32)
        outgoing[slot] = sent.astype(BF)
        for which, shift in enumerate(SHIFTS):

            @pl.when((sub + shift >= 0) & (sub + shift < n_sub))
            def _(which=which):
                robin_copy(slot, which).start()

        pl.when(step == 1)(rest_of_constants)

        field_copy(slot).wait_recv()
        both = jnp.concatenate([own, far_field[slot]], axis=0)
        total = [base[:, p * L : (p + 1) * L] for p in range(4)]
        for f in range(4):
            gathered = dot(near[pl.ds(f * L, L), :], both).astype(BF)
            flux = [dot(gathered[:, p * L : (p + 1) * L], face_t[f]) for p in range(4)]
            re, im = couple[f, 0], couple[f, 1]
            for s in range(2):
                total[2 * s] += re * flux[2 * s] - im * flux[2 * s + 1]
                total[2 * s + 1] += re * flux[2 * s + 1] + im * flux[2 * s]
        for p in range(4):
            at = pl.ds(p * L, L)
            others = [lifted[lax.rem(r + n, ROUNDS), :, at] for n in range(1, ROUNDS)]
            rhs[:, at] = total[p] + (others[0] + others[1] + others[2])

        for which, shift in enumerate(SHIFTS):

            @pl.when((sub - shift >= 0) & (sub - shift < n_sub))
            def _(which=which):
                robin_copy(slot, which).wait_recv()

        offset = jnp.broadcast_to(matching[0, r] - sub, square)
        arrived = jnp.zeros(square, BF).astype(F32)
        for which, shift in enumerate(SHIFTS):
            arrived = jnp.where(offset == -shift, arriving[slot, which].astype(F32), arrived)
        live = rows < counts[0, r]
        updated = jnp.where(live, arrived, former.astype(F32)).astype(BF)
        interface[r] = updated
        landed = dot(lift_hot[r], updated).astype(BF)
        side = jnp.concatenate([landed[f * L : (f + 1) * L] for f in range(4)], axis=1)
        added = dot(side, from_trace[...])
        lifted[r] = added
        lay_out(rhs[...] + added)
        pl.when(step > 1)(lambda: sent_all(1 - slot))

    def sent_all(slot):
        field_copy(slot).wait_send()
        for which, shift in enumerate(SHIFTS):

            @pl.when((sub + shift >= 0) & (sub + shift < n_sub))
            def _(which=which):
                robin_copy(slot, which).wait_send()

    def lay_out(value):
        for el in range(2):
            for c in range(2):
                for s in range(2):
                    p = 2 * s + c
                    left[el, pl.ds(el * 4 + c * 2 + s, half, stride=8), :] = value[
                        el * half : (el + 1) * half, p * L : (p + 1) * L
                    ]

    def advance(step, carry):
        pl.when(step > 0)(lambda: exchange(step))
        following = lax.rem(step + 1, 2)
        for pair in range(half):
            spot = pl.ds(pair * 8, 8)
            vector = jnp.concatenate([left[0, spot, :], left[1, spot, :]], axis=1).astype(BF)
            matrix = jnp.concatenate([weights[pair], weights[half + pair]], axis=0)
            result = dot(vector, matrix)
            product[0, spot, :] = result[:, 0:L]
            product[1, spot, :] = result[:, L : 2 * L]
        for el in range(2):
            for s in range(2):
                at = [pl.ds(el * 4 + c * 2 + s, half, stride=8) for c in range(2)]
                re = product[0, at[0], :] - product[1, at[1], :]
                im = product[1, at[0], :] + product[0, at[1], :]
                field[following, el * half : (el + 1) * half, 2 * s * L : (2 * s + 1) * L] = (
                    re.astype(BF)
                )
                field[following, el * half : (el + 1) * half, (2 * s + 1) * L : (2 * s + 2) * L] = (
                    im.astype(BF)
                )
        @pl.when(step < STEPS - 1)
        def _():
            field_copy(following).start()

        return carry

    lay_out(base[...])
    lax.fori_loop(0, STEPS, advance, 0)
    sent_all((STEPS - 1) % 2)
    final = STEPS % 2
    for s in range(2):
        for c in range(2):
            p = 2 * s + c
            turned = dot_nt(identity, field[final, :, p * L : (p + 1) * L])
            out[2 * c + s] = turned[0:DOF].astype(BF)


def shards(
    n_sub,
    source_terms,
    inverse_blocks,
    face_matrices,
    trace_matrices,
    neighbours,
    coupling,
    slot_faces,
    robin_params,
    matching,
    counts,
):
    square = (L, L)
    result = pl.pallas_call(
        functools.partial(kernel, n_sub),
        out_shape=jax.ShapeDtypeStruct((4, DOF, E_DEV), BF),
        in_specs=[pl.BlockSpec(memory_space=pl.ANY)] * 10,
        out_specs=pl.BlockSpec(memory_space=pltpu.VMEM),
        scratch_shapes=[
            pltpu.VMEM((DOF, 208, L), BF),
            pltpu.VMEM((DOF, 2, L), BF),
            pltpu.VMEM((2, 208, L), BF),
            pltpu.VMEM((2, 2, L), BF),
            pltpu.VMEM((512, L), F32),
            pltpu.VMEM((432, DOF), BF),
            pltpu.VMEM((4, DOF), BF),
            pltpu.VMEM((L, DOF), BF),
            pltpu.VMEM((2, 4, DOF), BF),
            pltpu.VMEM((4, L, L), BF),
            pltpu.VMEM((4, L), I32),
            pltpu.VMEM((4, 2, L), BF),
            pltpu.VMEM((4, L), I32),
            pltpu.VMEM((2, 4, L), BF),
            pltpu.SMEM((1, 4), I32),
            pltpu.SMEM((1, 4), I32),
            pltpu.VMEM((JP * PITCH + 8, L), F32),
            pltpu.VMEM((2, 2, 8 * E_DEV, L), F32),
            pltpu.VMEM((E_DEV, L, 2 * L), BF),
            pltpu.VMEM(square, BF),
            pltpu.VMEM((4 * L, 2 * L), BF),
            pltpu.VMEM((ROUNDS, L, 4 * L), BF),
            pltpu.VMEM((ROUNDS, 4 * L, L), BF),
            pltpu.VMEM((4 * L, 4 * L), BF),
            pltpu.VMEM((4 * L, 4 * L), BF),
            pltpu.VMEM((ROUNDS, L, L), F32),
            pltpu.VMEM((ROUNDS, L, L), F32),
            pltpu.VMEM((4, 2, L, L), F32),
            pltpu.VMEM((E_DEV, 4 * L), F32),
            pltpu.VMEM((ROUNDS, E_DEV, 4 * L), F32),
            pltpu.VMEM((ROUNDS, L, L), BF),
            pltpu.VMEM((E_DEV, 4 * L), F32),
            pltpu.VMEM((2, 4 * E_DEV, L), F32),
            pltpu.VMEM((2, 4 * E_DEV, L), F32),
            pltpu.VMEM((2, E_DEV, 4 * L), BF),
            pltpu.VMEM((2, E_DEV, 4 * L), BF),
            pltpu.VMEM((2, L, L), BF),
            pltpu.VMEM((2, 4, L, L), BF),
            pltpu.VMEM(square, BF),
            pltpu.VMEM((2 * L, 2 * L), BF),
            pltpu.SemaphoreType.DMA((13 + PARTS,)),
            pltpu.SemaphoreType.DMA((2,)),
            pltpu.SemaphoreType.DMA((2,)),
            pltpu.SemaphoreType.DMA((2, 4)),
            pltpu.SemaphoreType.DMA((2, 4)),
        ],
        compiler_params=pltpu.CompilerParams(
            collective_id=0, has_side_effects=True, vmem_limit_bytes=56 * 2**20
        ),
    )(
        jnp.transpose(inverse_blocks, (1, 2, 0, 3)),
        source_terms,
        jnp.transpose(face_matrices, (1, 0, 2)),
        jnp.transpose(trace_matrices, (1, 0, 2)),
        jnp.transpose(neighbours),
        jnp.transpose(coupling, (1, 2, 0)),
        slot_faces[0],
        robin_params[:, 0],
        jnp.transpose(matching),
        jnp.transpose(counts[:, :, 0]),
    )
    return result.reshape(2, 2, DOF, E_DEV).transpose(0, 2, 1, 3)


def solution(mesh):
    in_specs = (
        P(None, None, None, ("sub", "blk")),
        P(None, None, None, ("sub", "blk")),
        P(),
        P(),
        P(("sub", "blk"), None),
        P(("sub", "blk"), None, None),
        P("sub", None, "blk"),
        P(None, "sub", None, "blk"),
        P(None, "sub"),
        P(None, "sub", "blk"),
    )
    out_specs = P(None, None, None, ("sub", "blk"))
    body = functools.partial(shards, mesh.shape["sub"])
    return jax.shard_map(body, mesh=mesh, in_specs=in_specs, out_specs=out_specs, check_vma=False)
```

time: 100 us -> 76.1 us (0.76)
  Pallas kernels: 90.6 us -> 74.4 us
  local copies, waits for them, and re-layouts: 9.38 us -> 1.63 us
    pallas_call x1, Pallas kernels: 90.6 us -> 74.4 us  [shards(): pl.pallas_call(functools.partial(kernel, n_sub), out_shape=jax.ShapeDtype...]
    unnamed x7 -> x0, local copies, waits for them, and re-layouts: 4.89 us -> none
    squeeze x1 -> x0, local copies, waits for them, and re-layouts: 1.32 us -> none  [shards(): counts[:, :, 0]]
where the time goes in v2:
time: 76.1 us; the launch traced here: 76 us
  Pallas kernels  74.4 us (98%)
  local copies, waits for them, and re-layouts  1.63 us (2%)
    pallas_call x1, Pallas kernels, shards(): pl.pallas_call(functools.partial(kernel, n_sub), out_shape=jax.ShapeDtype...  74.4 us
    reshape x1, local copies, waits for them, and re-layouts, shards(): return result.reshape(2, 2, DOF, E_DEV).transpose(0, 2, 1, 3)  1.63 us

profile of v2, /device:TPU:6, one launch (start us, length us, event | category | flops | bytes accessed | tf_op | source)
XLA Modules:
  0.0 76.0 jit_solution(15060072947562820860)
XLA Ops:
  0.0 74.4 %shard_map.100 = bf16[4,105,128]{2,1,0:T(8,128)(2,1)} custom-call(bf16[105,105,2,128]{3,2,1,0:T(2,128)(2,1)} %bitcast.13, bf16[2,105,2,128]{3,2,1,0:T(2,128)(2,1)} %source.1, bf16[105,4,105]{2,1,0:T(4,128)(2,1)} %bitcast.15, bf16[30,4,105]{2,1,0:T(4,128)(2,1)} %bitcast.16, s32[4,128]{1,0:T(4,128)} %bitcast.17, bf16[4,2,128]{2,1,0:T(2,128)(2,1)} %bitcast.18, ...), custom_call_target="tpu_custom_call" | custom-call | tf_op jit(solution)/shard_map/pallas_call | solution.py:445
  74.4 1.6 %copy.13 = bf16[2,2,105,128]{3,1,2,0:T(2,128)(2,1)} copy(bf16[2,2,105,128]{3,2,1,0:T(8,128)(2,1)} %bitcast.14) | data formatting | bytes 215040 | tf_op jit(solution)/shard_map/reshape | solution.py:512

commit v3 on v2

--- a/solution.py
+++ b/solution.py
@@ -19,7 +19,6 @@
 L = 128
 JP = 112
 PITCH = 216
-PARTS = 3
 SHIFTS = (1, -1, 2, -2)
 NT = (((1,), (1,)), ((), ()))
 
@@ -98,6 +97,7 @@
     trace_n_ref,
     eye_wide,
     load_sem,
+    rows_sem,
     field_send,
     field_recv,
     robin_send,
@@ -109,29 +109,32 @@
     source_flat = source.reshape(2, 2 * DOF, L)
     face_flat = face.reshape(4 * DOF, DOF)
     loads = inverse.reshape(DOF, 2 * DOF, L)
-    small = [
+    def load_rows(group):
+        at = pl.ds(pl.multiple_of(group * 32, 32), 32)
+        return pltpu.make_async_copy(loads.at[:, at], packed.at[:, at], rows_sem.at[group])
+
+    moves = [
         (slots_in, slots),
         (robin_in, robin),
-        (neighbours_in, neighbours),
-        (coupling_in, coupling),
-        (matching_in, matching),
-        (counts_in, counts),
-    ]
-    moves = [
         (trace_flat.at[pl.ds(0, 112)], trace_rows.at[pl.ds(0, 112)]),
         (trace.at[pl.ds(28, 2)], trace_tail),
         (source_flat.at[:, pl.ds(0, 208)], source_rows),
         (source_flat.at[:, pl.ds(208, 2)], source_tail),
         (loads.at[:, pl.ds(208, 2)], tail),
+        (loads.at[:, pl.ds(192, 16)], packed.at[:, pl.ds(192, 16)]),
+        (neighbours_in, neighbours),
+        (coupling_in, coupling),
+        (matching_in, matching),
+        (counts_in, counts),
+        (face_flat.at[pl.ds(0, 416)], face_rows.at[pl.ds(0, 416)]),
+        (face.at[DOF - 1], face_tail),
     ]
-    for part in range(PARTS):
-        chunk = pl.ds(part * (DOF // PARTS), DOF // PARTS)
-        moves.append((loads.at[chunk, pl.ds(0, 208)], packed.at[chunk]))
-    moves.append((face_flat.at[pl.ds(0, 416)], face_rows.at[pl.ds(0, 416)]))
-    moves.append((face.at[DOF - 1], face_tail))
-    moves += small
     moves = [pltpu.make_async_copy(a, b, load_sem.at[n]) for n, (a, b) in enumerate(moves)]
-    for move in moves:
+    for move in moves[:6]:
+        move.start()
+    for group in range(6):
+        load_rows(group).start()
+    for move in moves[6:]:
         move.start()
     arriving[...] = jnp.zeros_like(arriving)
 
@@ -151,27 +154,26 @@
         barrier, inc=1, device_id=(sub, 1 - blk), device_id_type=pl.DeviceIdType.MESH
     )
 
+    half = E_DEV // 2
     square = (L, L)
     rows, lanes = iota(square, 0), iota(square, 1)
     eye[...] = hot(rows == lanes)
     identity = eye[...]
     eye_wide[...] = hot(iota((2 * L, 2 * L), 0) == iota((2 * L, 2 * L), 1))
-    left[...] = jnp.zeros_like(left)
-    lifted[...] = jnp.zeros_like(lifted)
+    left[1] = jnp.zeros((4 * E_DEV, L), F32)
     interface[...] = jnp.zeros_like(interface)
 
-    first_small = 7 + PARTS
-    for n in range(2):
-        moves[first_small + n].wait()
-    sign = jnp.where((lanes // 32) % 2 == 0, -2.0, 2.0)
-    for r in range(ROUNDS):
+    def slot_constants(r):
         code = jnp.broadcast_to(row(slots, r), square)
         for f in range(4):
             pick[r, :, pl.ds(f * L, L)] = dot_nt(identity, hot(code == 4 * rows + f)).astype(BF)
         robin_re[r] = 2.0 * dot_nt(identity, jnp.broadcast_to(row(robin, 0, r), square))
         robin_im[r] = sign * dot_nt(identity, jnp.broadcast_to(row(robin, 1, r), square))
-    moves[0].wait()
-    moves[1].wait()
+
+    sign = jnp.where((lanes // 32) % 2 == 0, -2.0, 2.0)
+    for move in moves[:4]:
+        move.wait()
+    slot_constants(1)
     last = trace_tail[...].astype(F32).reshape(8, DOF)
     trace_rows[112:128, :] = jnp.concatenate([last, jnp.zeros((8, DOF), F32)], axis=0).astype(BF)
     trace_n = dot(trace_rows[...], eye[0:DOF, :]).astype(BF)
@@ -182,8 +184,8 @@
         spread = hot((lane // L == kf % 4) & (lane % L == part * 32 + kf // 4))
         to_trace[pl.ds(part * L, L), :] = dot(trace_t, spread).astype(BF)
 
-    moves[2].wait()
-    moves[3].wait()
+    moves[4].wait()
+    moves[5].wait()
     for c in range(2):
         source_wide[pl.ds(c * 256, 208), :] = source_rows[c].astype(F32)
         source_wide[pl.ds(c * 256 + 208, 48), :] = jnp.concatenate(
@@ -193,9 +195,15 @@
         for c in range(2):
             p = 2 * s + c
             block = source_wide[pl.ds(c * 256 + s, L, stride=2), :].astype(BF)
+            block = jnp.concatenate([block[0:JP], block[96:JP]], axis=0)
             base[:, p * L : (p + 1) * L] = dot_nt(identity, block)
 
     def rest_of_constants():
+        for move in moves[8:]:
+            move.wait()
+        lifted[...] = jnp.zeros_like(lifted)
+        for r in (0, 2, 3):
+            slot_constants(r)
         for f in range(4):
             code = jnp.broadcast_to(row(neighbours, f), square)
             mine = hot(code == rows + blk * E_DEV)
@@ -211,47 +219,47 @@
             for f in range(4):
                 lift_hot[r, pl.ds(f * L, L), :] = hot((code == 4 * rows + f) & live)
         trow, tkf = iota((4 * L, L), 0), iota((4 * L, L), 1)
+        folded = jnp.where(lanes >= JP, lanes - 16, lanes)
+        repeated = dot(trace_n_ref[...], hot(rows == folded)).astype(BF)
         for part in range(4):
             spread = hot((trow // L == tkf % 4) & (trow % L == part * 32 + tkf // 4))
-            from_trace[:, pl.ds(part * L, L)] = dot(spread, trace_n_ref[...]).astype(BF)
+            from_trace[:, pl.ds(part * L, L)] = dot(spread, repeated).astype(BF)
         end = jnp.concatenate([face_tail[...].astype(F32), jnp.zeros((12, DOF), F32)], axis=0)
         face_rows[416:432, :] = end.astype(BF)
         frow, fk = iota((L, 432), 0), iota((L, 432), 1)
+        frow = jnp.where(frow >= JP, frow - 16, frow)
         for f in range(4):
             chosen = dot(hot(4 * frow + f == fk), face_rows[...]).astype(BF)
             face_t[f] = dot_nt(eye[:, 0:DOF], chosen).astype(BF)
 
     trace_n_ref[...] = trace_n
 
-    def clear(e, carry):
-        for q in range(8):
-            weights[e * 8 + q, JP:L, :] = jnp.zeros((L - JP, 2 * L), BF)
-        return carry
-
-    lax.fori_loop(0, E_DEV // 8, clear, 0)
     rest = (JP - DOF) * PITCH + 8
     wide[pl.ds(DOF * PITCH, rest), :] = jnp.zeros((rest, L), F32)
-    moves[4].wait()
-
-    def widen(chunk, carry):
-        for q in range(5):
-            i = chunk * 5 + q
-            start = pl.multiple_of(i * PITCH, 8)
-            wide[pl.ds(start, 208), :] = packed[i].astype(F32)
-            wide[pl.ds(pl.multiple_of(start + 208, 8), 8), :] = jnp.concatenate(
-                [tail[i].astype(F32), jnp.zeros((6, L), F32)], axis=0
-            )
-        return carry
-
-    each = DOF // PARTS // 5
-    for part in range(PARTS):
-        moves[5 + part].wait()
-        lax.fori_loop(part * each, (part + 1) * each, widen, 0)
-    for n in range(5 + PARTS, 7 + PARTS + len(small)):
-        if n not in (first_small, first_small + 1):
-            moves[n].wait()
-
-    def regroup(group, carry):
+
+    def regroup(group, final):
+        def widen(chunk, carry):
+            for q in range(15):
+                i = chunk * 15 + q
+                start = i * PITCH + group * 32
+                at = pl.multiple_of(group * 32, 32)
+                if final:
+                    end = jnp.concatenate([tail[i].astype(F32), jnp.zeros((6, L), F32)], axis=0)
+                    wide[pl.ds(pl.multiple_of(start, 8), 16), :] = packed[i, 192:208].astype(F32)
+                    wide[pl.ds(pl.multiple_of(start + 16, 8), 8), :] = end
+                else:
+                    wide[pl.ds(pl.multiple_of(start, 8), 32), :] = packed[i, pl.ds(at, 32)].astype(
+                        F32
+                    )
+            return carry
+
+        if final:
+            moves[6].wait()
+            moves[7].wait()
+        else:
+            load_rows(group).wait()
+        lax.fori_loop(0, DOF // 15, widen, 0)
+
         def block(inner, c):
             value = wide[pl.ds(group * 32 + 2 * inner + c, JP, stride=PITCH), :]
             return jnp.concatenate([value, jnp.zeros((L - JP, L), F32)], axis=0)
@@ -273,29 +281,35 @@
                 for c in range(2):
                     staged[c, inner // 8, pl.ds(inner % 8, E_DEV, stride=8), :] = turned[n][c]
 
-        def pack(chunk, inner_carry):
-            for q in range(16):
-                e = chunk * 16 + q
-                spot = pl.ds(pl.multiple_of(e * 8, 8), 8)
-                for c in range(2):
-                    tile = jnp.concatenate([staged[c, 0, spot, :], staged[c, 1, spot, :]], axis=0)
-                    weights[e, pl.ds(pl.multiple_of(group * 16, 16), 16), c * L : (c + 1) * L] = (
-                        tile.astype(BF)
-                    )
-            return inner_carry
-
-        lax.fori_loop(0, E_DEV // 16, pack, 0)
+        for later in range(2):
+            place = lax.rem(group + later, JP // 16) if not final else (1 - later) * group
+            at = pl.ds(pl.multiple_of(place * 16, 16), 16)
+
+            def pack(chunk, inner_carry, at=at):
+                for q in range(16):
+                    e = chunk * 16 + q
+                    spot = pl.ds(pl.multiple_of(e * 8, 8), 8)
+                    for c in range(2):
+                        tile = jnp.concatenate(
+                            [staged[c, 0, spot, :], staged[c, 1, spot, :]], axis=0
+                        )
+                        weights[e, at, c * L : (c + 1) * L] = tile.astype(BF)
+                return inner_carry
+
+            lax.fori_loop(later * half // 16, (later + 1) * half // 16, pack, 0)
+
+    def regroup_step(group, carry):
+        regroup(group, False)
         return carry
 
-    lax.fori_loop(0, JP // 16, regroup, 0)
+    lax.fori_loop(0, JP // 16 - 1, regroup_step, 0)
+    regroup(JP // 16 - 1, True)
 
     neighbours_there = jnp.int32(1)
     for shift in SHIFTS:
         there = (sub + shift >= 0) & (sub + shift < n_sub)
         neighbours_there = neighbours_there + there.astype(I32)
     pl.semaphore_wait(barrier, neighbours_there)
-
-    half = E_DEV // 2
 
     def field_copy(slot):
         return pltpu.make_async_remote_copy(
@@ -382,20 +396,22 @@
                 robin_copy(slot, which).wait_send()
 
     def lay_out(value):
-        for el in range(2):
-            for c in range(2):
-                for s in range(2):
-                    p = 2 * s + c
-                    left[el, pl.ds(el * 4 + c * 2 + s, half, stride=8), :] = value[
-                        el * half : (el + 1) * half, p * L : (p + 1) * L
-                    ]
+        later = iota((half, L), 1) >= JP
+        for c in range(2):
+            for s in range(2):
+                p = 2 * s + c
+                first = value[0:half, p * L : (p + 1) * L]
+                second = value[half:E_DEV, p * L : (p + 1) * L]
+                left[0, pl.ds(c * 2 + s, half, stride=8), :] = jnp.where(later, 0.0, first)
+                left[0, pl.ds(4 + c * 2 + s, half, stride=8), :] = jnp.where(later, second, 0.0)
+                left[1, pl.ds(4 + c * 2 + s, half, stride=8), :] = second
 
     def advance(step, carry):
         pl.when(step > 0)(lambda: exchange(step))
         following = lax.rem(step + 1, 2)
         for pair in range(half):
             spot = pl.ds(pair * 8, 8)
-            vector = jnp.concatenate([left[0, spot, :], left[1, spot, :]], axis=1).astype(BF)
+            vector = jnp.concatenate([left[0, spot, :], left[1, spot, 0:96]], axis=1).astype(BF)
             matrix = jnp.concatenate([weights[pair], weights[half + pair]], axis=0)
             result = dot(vector, matrix)
             product[0, spot, :] = result[:, 0:L]
@@ -466,7 +482,7 @@
             pltpu.SMEM((1, 4), I32),
             pltpu.VMEM((JP * PITCH + 8, L), F32),
             pltpu.VMEM((2, 2, 8 * E_DEV, L), F32),
-            pltpu.VMEM((E_DEV, L, 2 * L), BF),
+            pltpu.VMEM((E_DEV, JP, 2 * L), BF),
             pltpu.VMEM(square, BF),
             pltpu.VMEM((4 * L, 2 * L), BF),
             pltpu.VMEM((ROUNDS, L, 4 * L), BF),
@@ -488,7 +504,8 @@
             pltpu.VMEM((2, 4, L, L), BF),
             pltpu.VMEM(square, BF),
             pltpu.VMEM((2 * L, 2 * L), BF),
-            pltpu.SemaphoreType.DMA((13 + PARTS,)),
+            pltpu.SemaphoreType.DMA((14,)),
+            pltpu.SemaphoreType.DMA((6,)),
             pltpu.SemaphoreType.DMA((2,)),
             pltpu.SemaphoreType.DMA((2,)),
             pltpu.SemaphoreType.DMA((2, 4)),

time: 76.1 us -> 73.5 us (0.966)
  Pallas kernels: 74.4 us -> 71.8 us
    pallas_call x1, Pallas kernels: 74.4 us -> 71.8 us  [shards(): pl.pallas_call(functools.partial(kernel, n_sub), out_shape=jax.ShapeDtype...]
where the time goes in v3:
time: 73.5 us; the launch traced here: 73.4 us
  Pallas kernels  71.8 us (98%)
  local copies, waits for them, and re-layouts  1.63 us (2%)
    pallas_call x1, Pallas kernels, shards(): pl.pallas_call(functools.partial(kernel, n_sub), out_shape=jax.ShapeDtype...  71.8 us
    reshape x1, local copies, waits for them, and re-layouts, shards(): return result.reshape(2, 2, DOF, E_DEV).transpose(0, 2, 1, 3)  1.63 us

profile of v3, /device:TPU:6, one launch (start us, length us, event | category | flops | bytes accessed | tf_op | source)
XLA Modules:
  0.0 73.4 jit_solution(1948691744559435575)
XLA Ops:
  0.0 71.8 %shard_map.100 = bf16[4,105,128]{2,1,0:T(8,128)(2,1)} custom-call(bf16[105,105,2,128]{3,2,1,0:T(2,128)(2,1)} %bitcast.13, bf16[2,105,2,128]{3,2,1,0:T(2,128)(2,1)} %source.1, bf16[105,4,105]{2,1,0:T(4,128)(2,1)} %bitcast.15, bf16[30,4,105]{2,1,0:T(4,128)(2,1)} %bitcast.16, s32[4,128]{1,0:T(4,128)} %bitcast.17, bf16[4,2,128]{2,1,0:T(2,128)(2,1)} %bitcast.18, ...), custom_call_target="tpu_custom_call" | custom-call | tf_op jit(solution)/shard_map/pallas_call | solution.py:461
  71.8 1.6 %copy.13 = bf16[2,2,105,128]{3,1,2,0:T(2,128)(2,1)} copy(bf16[2,2,105,128]{3,2,1,0:T(8,128)(2,1)} %bitcast.14) | data formatting | bytes 215040 | tf_op jit(solution)/shard_map/reshape | solution.py:529

commit v4 on v3

--- a/solution.py
+++ b/solution.py
@@ -19,7 +19,7 @@
 L = 128
 JP = 112
 PITCH = 216
-SHIFTS = (1, -1, 2, -2)
+SHIFTS = (2, -2, 1, -1)
 NT = (((1,), (1,)), ((), ()))
 
 
@@ -237,29 +237,26 @@
     rest = (JP - DOF) * PITCH + 8
     wide[pl.ds(DOF * PITCH, rest), :] = jnp.zeros((rest, L), F32)
 
-    def regroup(group, final):
-        def widen(chunk, carry):
+    def widen(group):
+        at = pl.ds(pl.multiple_of(group * 32, 32), 32)
+        for i in range(DOF):
+            start = pl.multiple_of(i * PITCH + group * 32, 8)
+            wide[pl.ds(start, 32), :] = packed[i, at].astype(F32)
+
+    def add_tails():
+        moves[6].wait()
+        moves[7].wait()
+
+        def add_tail(chunk, carry):
             for q in range(15):
                 i = chunk * 15 + q
-                start = i * PITCH + group * 32
-                at = pl.multiple_of(group * 32, 32)
-                if final:
-                    end = jnp.concatenate([tail[i].astype(F32), jnp.zeros((6, L), F32)], axis=0)
-                    wide[pl.ds(pl.multiple_of(start, 8), 16), :] = packed[i, 192:208].astype(F32)
-                    wide[pl.ds(pl.multiple_of(start + 16, 8), 8), :] = end
-                else:
-                    wide[pl.ds(pl.multiple_of(start, 8), 32), :] = packed[i, pl.ds(at, 32)].astype(
-                        F32
-                    )
+                end = jnp.concatenate([tail[i].astype(F32), jnp.zeros((14, L), F32)], axis=0)
+                packed[i, 208:224] = end.astype(BF)
             return carry
 
-        if final:
-            moves[6].wait()
-            moves[7].wait()
-        else:
-            load_rows(group).wait()
-        lax.fori_loop(0, DOF // 15, widen, 0)
-
+        lax.fori_loop(0, DOF // 15, add_tail, 0)
+
+    def regroup(group, final):
         def block(inner, c):
             value = wide[pl.ds(group * 32 + 2 * inner + c, JP, stride=PITCH), :]
             return jnp.concatenate([value, jnp.zeros((L - JP, L), F32)], axis=0)
@@ -281,27 +278,25 @@
                 for c in range(2):
                     staged[c, inner // 8, pl.ds(inner % 8, E_DEV, stride=8), :] = turned[n][c]
 
+        if not final:
+            widen(group + 1)
         for later in range(2):
             place = lax.rem(group + later, JP // 16) if not final else (1 - later) * group
             at = pl.ds(pl.multiple_of(place * 16, 16), 16)
-
-            def pack(chunk, inner_carry, at=at):
-                for q in range(16):
-                    e = chunk * 16 + q
-                    spot = pl.ds(pl.multiple_of(e * 8, 8), 8)
-                    for c in range(2):
-                        tile = jnp.concatenate(
-                            [staged[c, 0, spot, :], staged[c, 1, spot, :]], axis=0
-                        )
-                        weights[e, at, c * L : (c + 1) * L] = tile.astype(BF)
-                return inner_carry
-
-            lax.fori_loop(later * half // 16, (later + 1) * half // 16, pack, 0)
+            for e in range(later * half, (later + 1) * half):
+                spot = pl.ds(e * 8, 8)
+                for c in range(2):
+                    tile = jnp.concatenate([staged[c, 0, spot, :], staged[c, 1, spot, :]], axis=0)
+                    weights[e, at, c * L : (c + 1) * L] = tile.astype(BF)
 
     def regroup_step(group, carry):
+        pl.when(group < 5)(lambda: load_rows(group + 1).wait())
+        pl.when(group == 5)(add_tails)
         regroup(group, False)
         return carry
 
+    load_rows(0).wait()
+    widen(0)
     lax.fori_loop(0, JP // 16 - 1, regroup_step, 0)
     regroup(JP // 16 - 1, True)
 
@@ -351,6 +346,7 @@
                 robin_copy(slot, which).start()
 
         pl.when(step == 1)(rest_of_constants)
+        pl.when(step > 1)(lambda: sent_all(1 - slot))
 
         field_copy(slot).wait_recv()
         both = jnp.concatenate([own, far_field[slot]], axis=0)
@@ -385,7 +381,6 @@
         added = dot(side, from_trace[...])
         lifted[r] = added
         lay_out(rhs[...] + added)
-        pl.when(step > 1)(lambda: sent_all(1 - slot))
 
     def sent_all(slot):
         field_copy(slot).wait_send()
@@ -409,24 +404,26 @@
     def advance(step, carry):
         pl.when(step > 0)(lambda: exchange(step))
         following = lax.rem(step + 1, 2)
-        for pair in range(half):
-            spot = pl.ds(pair * 8, 8)
-            vector = jnp.concatenate([left[0, spot, :], left[1, spot, 0:96]], axis=1).astype(BF)
-            matrix = jnp.concatenate([weights[pair], weights[half + pair]], axis=0)
-            result = dot(vector, matrix)
-            product[0, spot, :] = result[:, 0:L]
-            product[1, spot, :] = result[:, L : 2 * L]
-        for el in range(2):
-            for s in range(2):
-                at = [pl.ds(el * 4 + c * 2 + s, half, stride=8) for c in range(2)]
-                re = product[0, at[0], :] - product[1, at[1], :]
-                im = product[1, at[0], :] + product[0, at[1], :]
-                field[following, el * half : (el + 1) * half, 2 * s * L : (2 * s + 1) * L] = (
-                    re.astype(BF)
-                )
-                field[following, el * half : (el + 1) * half, (2 * s + 1) * L : (2 * s + 2) * L] = (
-                    im.astype(BF)
-                )
+        for part in range(4):
+            size = half // 4
+            for pair in range(part * size, (part + 1) * size):
+                spot = pl.ds(pair * 8, 8)
+                vector = jnp.concatenate([left[0, spot, :], left[1, spot, 0:96]], axis=1).astype(BF)
+                matrix = jnp.concatenate([weights[pair], weights[half + pair]], axis=0)
+                result = dot(vector, matrix)
+                product[0, spot, :] = result[:, 0:L]
+                product[1, spot, :] = result[:, L : 2 * L]
+            for el in range(2):
+                at = pl.ds(el * half + part * size, size)
+                for s in range(2):
+                    first = part * size * 8 + el * 4 + s
+                    pick_re = pl.ds(first, size, stride=8)
+                    pick_im = pl.ds(first + 2, size, stride=8)
+                    re = product[0, pick_re, :] - product[1, pick_im, :]
+                    im = product[1, pick_re, :] + product[0, pick_im, :]
+                    field[following, at, 2 * s * L : (2 * s + 1) * L] = re.astype(BF)
+                    field[following, at, (2 * s + 1) * L : (2 * s + 2) * L] = im.astype(BF)
+
         @pl.when(step < STEPS - 1)
         def _():
             field_copy(following).start()
@@ -464,7 +461,7 @@
         in_specs=[pl.BlockSpec(memory_space=pl.ANY)] * 10,
         out_specs=pl.BlockSpec(memory_space=pltpu.VMEM),
         scratch_shapes=[
-            pltpu.VMEM((DOF, 208, L), BF),
+            pltpu.VMEM((DOF, 224, L), BF),
             pltpu.VMEM((DOF, 2, L), BF),
             pltpu.VMEM((2, 208, L), BF),
             pltpu.VMEM((2, 2, L), BF),

time: 73.5 us -> 72.7 us (0.989)
  Pallas kernels: 71.8 us -> 70.9 us
    pallas_call x1, Pallas kernels: 71.8 us -> 70.9 us  [shards(): pl.pallas_call(functools.partial(kernel, n_sub), out_shape=jax.ShapeDtype...]
where the time goes in v4:
time: 72.7 us; the launch traced here: 72.6 us
  Pallas kernels  70.9 us (98%)
  local copies, waits for them, and re-layouts  1.63 us (2%)
    pallas_call x1, Pallas kernels, shards(): pl.pallas_call(functools.partial(kernel, n_sub), out_shape=jax.ShapeDtype...  70.9 us
    reshape x1, local copies, waits for them, and re-layouts, shards(): return result.reshape(2, 2, DOF, E_DEV).transpose(0, 2, 1, 3)  1.63 us

profile of v4, /device:TPU:6, one launch (start us, length us, event | category | flops | bytes accessed | tf_op | source)
XLA Modules:
  0.0 72.6 jit_solution(13919358112317735971)
XLA Ops:
  0.0 70.9 %shard_map.100 = bf16[4,105,128]{2,1,0:T(8,128)(2,1)} custom-call(bf16[105,105,2,128]{3,2,1,0:T(2,128)(2,1)} %bitcast.13, bf16[2,105,2,128]{3,2,1,0:T(2,128)(2,1)} %source.1, bf16[105,4,105]{2,1,0:T(4,128)(2,1)} %bitcast.15, bf16[30,4,105]{2,1,0:T(4,128)(2,1)} %bitcast.16, s32[4,128]{1,0:T(4,128)} %bitcast.17, bf16[4,2,128]{2,1,0:T(2,128)(2,1)} %bitcast.18, ...), custom_call_target="tpu_custom_call" | custom-call | tf_op jit(solution)/shard_map/pallas_call | solution.py:458
  70.9 1.6 %copy.13 = bf16[2,2,105,128]{3,1,2,0:T(2,128)(2,1)} copy(bf16[2,2,105,128]{3,2,1,0:T(8,128)(2,1)} %bitcast.14) | data formatting | bytes 215040 | tf_op jit(solution)/shard_map/reshape | solution.py:526

commit v5 on v4

--- a/solution.py
+++ b/solution.py
@@ -326,7 +326,7 @@
             device_id_type=pl.DeviceIdType.MESH,
         )
 
-    def exchange(step):
+    def prepare(step):
         slot = lax.rem(step, 2)
         r = lax.rem(step, ROUNDS)
         own = field[slot]
@@ -339,12 +339,21 @@
         former = interface[r]
         sent = robin_re[r] * traced + robin_im[r] * turned - former.astype(F32)
         outgoing[slot] = sent.astype(BF)
+
+    def send_all(slot):
         for which, shift in enumerate(SHIFTS):
 
             @pl.when((sub + shift >= 0) & (sub + shift < n_sub))
             def _(which=which):
                 robin_copy(slot, which).start()
 
+        field_copy(slot).start()
+
+    def exchange(step):
+        slot = lax.rem(step, 2)
+        r = lax.rem(step, ROUNDS)
+        own = field[slot]
+        former = interface[r]
         pl.when(step == 1)(rest_of_constants)
         pl.when(step > 1)(lambda: sent_all(1 - slot))
 
@@ -401,7 +410,7 @@
                 left[0, pl.ds(4 + c * 2 + s, half, stride=8), :] = jnp.where(later, second, 0.0)
                 left[1, pl.ds(4 + c * 2 + s, half, stride=8), :] = second
 
-    def advance(step, carry):
+    def advance(step, carry, ends=False):
         pl.when(step > 0)(lambda: exchange(step))
         following = lax.rem(step + 1, 2)
         for part in range(4):
@@ -424,14 +433,15 @@
                     field[following, at, 2 * s * L : (2 * s + 1) * L] = re.astype(BF)
                     field[following, at, (2 * s + 1) * L : (2 * s + 2) * L] = im.astype(BF)
 
-        @pl.when(step < STEPS - 1)
-        def _():
-            field_copy(following).start()
+        if not ends:
+            prepare(step + 1)
+            send_all(following)
 
         return carry
 
     lay_out(base[...])
-    lax.fori_loop(0, STEPS, advance, 0)
+    lax.fori_loop(0, STEPS - 1, advance, 0)
+    advance(jnp.int32(STEPS - 1), 0, ends=True)
     sent_all((STEPS - 1) % 2)
     final = STEPS % 2
     for s in range(2):

time: 72.7 us -> 72.3 us (level)
  no operation moved by 1% of the time
where the time goes in v5:
time: 72.3 us; the launch traced here: 72.2 us
  Pallas kernels  70.5 us (98%)
  local copies, waits for them, and re-layouts  1.63 us (2%)
    pallas_call x1, Pallas kernels, shards(): pl.pallas_call(functools.partial(kernel, n_sub), out_shape=jax.ShapeDtype...  70.5 us
    reshape x1, local copies, waits for them, and re-layouts, shards(): return result.reshape(2, 2, DOF, E_DEV).transpose(0, 2, 1, 3)  1.63 us

profile of v5, /device:TPU:6, one launch (start us, length us, event | category | flops | bytes accessed | tf_op | source)
XLA Modules:
  0.0 72.2 jit_solution(1264013943960993920)
XLA Ops:
  0.0 70.5 %shard_map.100 = bf16[4,105,128]{2,1,0:T(8,128)(2,1)} custom-call(bf16[105,105,2,128]{3,2,1,0:T(2,128)(2,1)} %bitcast.13, bf16[2,105,2,128]{3,2,1,0:T(2,128)(2,1)} %source.1, bf16[105,4,105]{2,1,0:T(4,128)(2,1)} %bitcast.15, bf16[30,4,105]{2,1,0:T(4,128)(2,1)} %bitcast.16, s32[4,128]{1,0:T(4,128)} %bitcast.17, bf16[4,2,128]{2,1,0:T(2,128)(2,1)} %bitcast.18, ...), custom_call_target="tpu_custom_call" | custom-call | tf_op jit(solution)/shard_map/pallas_call | solution.py:468
  70.6 1.6 %copy.13 = bf16[2,2,105,128]{3,1,2,0:T(2,128)(2,1)} copy(bf16[2,2,105,128]{3,2,1,0:T(8,128)(2,1)} %bitcast.14) | data formatting | bytes 215040 | tf_op jit(solution)/shard_map/reshape | solution.py:536
